TPU v7x, 512 devices: a whole 4x4x16 slice. The times are simulated.
512 devices in a mesh: modes: 16 (over y, x_lo, core), sites: 32 (over x_hi, z).
Axes of the slice: x: 4 (x_hi: 2, x_lo: 2; x = x_hi * 2 + x_lo), y: 4, z: 16, core: 2. Of those that a mesh axis runs over, the one named last changes fastest.
Arguments:
- wave_state: float32 [4, 128, 131072], P(None, 'modes', 'sites'), may hold values from -6 to 6
- potential: float32 [131072], P('sites'), may hold values from -0.5 to 0.5
- spin_angle: float32 [131072], P('sites'), may hold values from -3.140625 to 3.140625
- magnet: float32 [3, 131072], P(None, 'sites'), may hold values from -0.6 to 0.6
- magnetic_mask: int32 [131072], P('sites'), may hold values 0 or 1
- mode_weight: float32 [128], P('modes'), may hold values from 0.5 to 2
- source_amp: float32 [4, 128], P(None, 'modes'), may hold values from -6 to 6
- mode_group: int32 [128], P('modes'), may hold values from 0 to 7
- energies: float32 [8], replicated, may hold values from -2 to 2
- lead_site: int32 [128], P('modes'), may hold values from 0 to 131071
Outputs:
- next_state: float32 [4, 128, 131072], P(None, 'modes', 'sites')
- densities: float32 [5, 131072], P(None, 'sites')
- magnet_next: float32 [3, 131072], P(None, 'sites')
All inputs are finite; a program needn't handle non-finite values. No bound on the sum of `magnetic_mask` on one device may be relied on, other than what follows from the above.
Results may differ from a plain program's by a relative error of at most 0.0001.
Values sent between devices are 32-bit elements; how exact they have to be, the bound alone decides.
A program may use at most 64 MiB of HBM per device.

v0:
```python
import math

import jax
import jax.numpy as jnp
from jax import lax
from jax.sharding import PartitionSpec as P

time_step = 0.6
start_time = 10.0
exchange_coupling = 0.5


def extended(cells, sides, width):
    for axis, dim in sides:
        count = lax.axis_size(axis)
        ends = count - 1
        head = lax.slice_in_dim(cells, 0, width, axis=dim)
        tail = lax.slice_in_dim(cells, cells.shape[dim] - width, cells.shape[dim], axis=dim)
        cells = jnp.concatenate(
            [
                lax.ppermute(tail, axis, [(i, (i + 1) % count) for i in range(ends)]),
                cells,
                lax.ppermute(head, axis, [((i + 1) % count, i) for i in range(ends)]),
            ],
            axis=dim,
        )
    return cells


def rotate_back(spinor, cosine, sine_term):
    shaped = spinor.reshape((2, 2) + spinor.shape[1:])
    spin_up = shaped[:, 0]
    spin_down = shaped[:, 1]
    turned = jnp.stack(
        [cosine * spin_up + sine_term * spin_down, cosine * spin_down - sine_term * spin_up], axis=1
    )
    return turned.reshape(spinor.shape)


def rotate_fore(spinor, cosine, sine_term):
    shaped = spinor.reshape((2, 2) + spinor.shape[1:])
    spin_up = shaped[:, 0]
    spin_down = shaped[:, 1]
    turned = jnp.stack(
        [cosine * spin_up - sine_term * spin_down, sine_term * spin_up + cosine * spin_down], axis=1
    )
    return turned.reshape(spinor.shape)


def exchange_term(spinor, sd_field):
    up_real, down_real, up_imag, down_imag = (spinor[0], spinor[1], spinor[2], spinor[3])
    field_x, field_y, field_z = (sd_field[0], sd_field[1], sd_field[2])
    out_up_real = field_z * up_real + field_x * down_real + field_y * down_imag
    out_down_real = field_x * up_real - field_y * up_imag - field_z * down_real
    out_up_imag = field_z * up_imag + field_x * down_imag - field_y * down_real
    out_down_imag = field_x * up_imag + field_y * up_real - field_z * down_imag
    return jnp.stack([out_up_real, out_down_real, out_up_imag, out_down_imag])


def source_field(offset, amplitude, energy, region):
    phase_angle = energy * (start_time + offset)
    cosine_phase = jnp.cos(phase_angle)
    sine_phase = jnp.sin(phase_angle)
    amp_real = amplitude[0:2]
    amp_imag = amplitude[2:4]
    real_part = amp_real * cosine_phase + amp_imag * sine_phase
    imag_part = amp_imag * cosine_phase - amp_real * sine_phase
    joined = jnp.concatenate([real_part, imag_part], axis=0)
    return joined[:, :, None] * region[None]


def rate(spinor, left_w, right_w, cosine, sine_term, potential, sd_field, source):
    hamil_term = (
        potential * spinor
        + exchange_term(spinor, sd_field)
        - rotate_fore(left_w + right_w, cosine, sine_term)
        + source
    )
    return jnp.concatenate([hamil_term[2:], -hamil_term[:2]], axis=0)


def densities_of(spinor, right_w, cosine, sine_term, weight_vec):
    up_real, down_real, up_imag, down_imag = (spinor[0], spinor[1], spinor[2], spinor[3])
    hopped = rotate_fore(right_w, cosine, sine_term)
    charge = up_real * up_real + down_real * down_real + up_imag * up_imag + down_imag * down_imag
    spin_x = 2.0 * (up_real * down_real + up_imag * down_imag)
    spin_y = 2.0 * (up_real * down_imag - up_imag * down_real)
    spin_z = up_real * up_real + up_imag * up_imag - down_real * down_real - down_imag * down_imag
    current = 2.0 * (
        up_real * hopped[2] + down_real * hopped[3] - up_imag * hopped[0] - down_imag * hopped[1]
    )
    stacked = jnp.stack([charge, spin_x, spin_y, spin_z, current])
    return jnp.sum(stacked * weight_vec[None, :, None], axis=1)


def advance(magnet, mask_float, totals):
    field_h = exchange_coupling * totals[1:4]
    torque = jnp.stack(
        [
            magnet[1] * field_h[2] - magnet[2] * field_h[1],
            magnet[2] * field_h[0] - magnet[0] * field_h[2],
            magnet[0] * field_h[1] - magnet[1] * field_h[0],
        ]
    )
    return magnet - time_step * (mask_float * torque)


def source_region(positions, lead_site, region_span):
    return (
        (positions[None, :] >= lead_site[:, None])
        & (positions[None, :] < lead_site[:, None] + region_span)
    ).astype(jnp.float32)


def local(
    wave_state,
    potential,
    spin_angle,
    magnet,
    magnetic_mask,
    mode_weight,
    source_amp,
    mode_group,
    energies,
    lead_site,
):
    local_sites = wave_state.shape[2]
    local_modes = wave_state.shape[1]
    site_count = lax.axis_size("sites")
    mode_count = lax.axis_size("modes")
    first_site = lax.axis_index("sites") * local_sites
    wire_sites = local_sites * site_count
    region_span = wire_sites // 8
    all_modes = local_modes * mode_count
    mask_float = magnetic_mask.astype(jnp.float32)
    group_ids = jnp.arange(energies.shape[0], dtype=jnp.int32)
    mode_energy = jnp.sum(
        jnp.where(
            mode_group[:, None] == group_ids[None, :],
            energies[None, :],
            jnp.zeros_like(energies)[None, :],
        ),
        axis=1,
    )
    cosine = jnp.cos(spin_angle)
    sine_term = jnp.sin(spin_angle)
    positions = first_site + jnp.arange(local_sites, dtype=jnp.int32)
    region = source_region(positions, lead_site, region_span)
    sd_field = exchange_coupling * mask_float * magnet

    def slope(spin_state, offset):
        weighted = rotate_back(spin_state, cosine, sine_term)
        padded = extended(weighted, (("sites", 2),), 1)
        source = source_field(offset, source_amp, mode_energy, region)
        return (
            rate(
                spin_state,
                padded[..., :-2],
                padded[..., 2:],
                cosine,
                sine_term,
                potential,
                sd_field,
                source,
            ),
            padded,
        )

    slope_one, padded_one = slope(wave_state, 0.0)
    slope_two, ignored = slope(wave_state + 0.5 * time_step * slope_one, 0.5 * time_step)
    slope_three, ignored = slope(wave_state + 0.5 * time_step * slope_two, 0.5 * time_step)
    slope_four, ignored = slope(wave_state + time_step * slope_three, time_step)
    next_state = wave_state + time_step / 6.0 * (
        slope_one + 2.0 * slope_two + 2.0 * slope_three + slope_four
    )
    right_w = padded_one[..., 2:]
    root_scale = 1.0 / math.sqrt(all_modes)
    row_scale = jnp.array(
        [1.0 / all_modes, root_scale, root_scale, root_scale, root_scale], jnp.float32
    )
    partial_value = (
        densities_of(wave_state, right_w, cosine, sine_term, mode_weight) * row_scale[:, None]
    )
    totals = lax.psum(partial_value, "modes")
    magnet_next = advance(magnet, mask_float, totals)
    return (next_state, totals, magnet_next)


def solution(mesh):
    return jax.shard_map(
        local,
        mesh=mesh,
        in_specs=(
            P(None, "modes", "sites"),
            P("sites"),
            P("sites"),
            P(None, "sites"),
            P("sites"),
            P("modes"),
            P(None, "modes"),
            P("modes"),
            P(),
            P("modes"),
        ),
        out_specs=(P(None, "modes", "sites"), P(None, "sites"), P(None, "sites")),
        check_vma=False,
    )
```

profile of v0, /device:TPU:1, one launch (start us, length us, event | category | flops | bytes accessed | tf_op | source)
XLA Modules:
  0.0 178.2 jit_solution(14860616858366607334)
XLA Ops:
  7.2 0.8 fusion.28
  8.0 1.1 multiply_add_fusion.13
  9.2 4.5 %collective-permute-start = (f32[4,8,1]{2,1,0:T(8,128)S(1)}, f32[4,8,1]{2,1,0:T(8,128)S(1)}, u32[]{:S(2)}, u32[]{:S(2)}) collective-permute-start(f32[4,8,1]{2,1,0:T(8,128)S(1)} %get-tuple-element.55), channel_id=1, source_target_pairs={{0,1},{1,2},{2,3},{3,4},{4,5},{5,6},{6,7},{7,8},{8,9},{9,10},{10,1... | collective-permute-start | bytes 392 | tf_op jit(solution)/shard_map/ppermute | solution.py:21
  13.7 1.3 collective-permute-start.1
  15.2 0.1 multiply_add_fusion.17
  15.4 0.6 copy-done.13
  16.0 0.2 select_reduce_fusion
  16.3 0.6 copy-done.10
  17.0 0.1 and_convert_fusion
  17.1 0.7 copy-done.9
  17.7 0.6 pad_maximum_fusion.20
  18.3 0.6 pad_maximum_fusion.22
  18.9 0.6 convert_element_type.10
  19.5 0.3 pad_maximum_fusion.6
  19.9 0.1 multiply_subtract_fusion
  20.1 0.6 copy-done.3
  20.7 0.1 fusion.5
  21.0 0.1 multiply_add_fusion.16
  21.2 0.7 fusion.24
  21.9 4.8 %collective-permute-start.2 = (f32[4,8,1]{2,1,0:T(8,128)}, f32[4,8,1]{2,1,0:T(8,128)}, u32[]{:S(2)}, u32[]{:S(2)}) collective-permute-start(f32[4,8,1]{2,1,0:T(8,128)} %get-tuple-element.50), channel_id=1, source_target_pairs={{0,1},{1,2},{2,3},{3,4},{4,5},{5,6},{6,7},{7,8},{8,9},{9,10},{10,1... | collective-permute-start | bytes 392 | tf_op jit(solution)/shard_map/ppermute | solution.py:21
  26.6 1.3 collective-permute-start.3
  28.0 0.6 copy-done.12
  28.6 0.3 multiply_reduce_fusion
  28.8 0.4 copy-done.11
  29.2 0.7 broadcast_multiply_fusion
  30.0 1.4 collective-permute-done.3
  31.4 1.1 fusion.2
  32.6 0.7 copy-done.4
  33.3 0.1 multiply_add_fusion.1
  33.7 4.4 %collective-permute-start.4 = (f32[4,8,1]{2,1,0:T(8,128)S(1)}, f32[4,8,1]{2,1,0:T(8,128)S(1)}, u32[]{:S(2)}, u32[]{:S(2)}) collective-permute-start(f32[4,8,1]{2,1,0:T(8,128)S(1)} %get-tuple-element.46), channel_id=1, source_target_pairs={{0,1},{1,2},{2,3},{3,4},{4,5},{5,6},{6,7},{7,8},{8,9},{9,10},{10,1... | collective-permute-start | bytes 392 | tf_op jit(solution)/shard_map/ppermute | solution.py:21
  38.1 1.3 collective-permute-start.5
  39.4 0.1 multiply_add_fusion.15
  39.5 4.3 %collective-permute-done.5 = f32[4,8,1]{2,1,0:T(8,128)S(1)} collective-permute-done((f32[4,8,1]{2,1,0:T(8,128)S(1)}, f32[4,8,1]{2,1,0:T(8,128)S(1)}, u32[]{:S(2)}, u32[]{:S(2)}) %collective-permute-start.5) | collective-permute-done | bytes 160 | tf_op jit(solution)/shard_map/ppermute | solution.py:23
  43.8 0.3 fusion.1
  44.3 0.1 multiply_add_fusion
  44.7 4.6 %collective-permute-start.6 = (f32[4,8,1]{2,1,0:T(8,128)S(1)}, f32[4,8,1]{2,1,0:T(8,128)S(1)}, u32[]{:S(2)}, u32[]{:S(2)}) collective-permute-start(f32[4,8,1]{2,1,0:T(8,128)S(1)} %get-tuple-element.42), channel_id=1, source_target_pairs={{0,1},{1,2},{2,3},{3,4},{4,5},{5,6},{6,7},{7,8},{8,9},{9,10},{10,1... | collective-permute-start | bytes 392 | tf_op jit(solution)/shard_map/ppermute | solution.py:21
  49.3 1.3 collective-permute-start.7
  50.6 0.1 multiply_add_fusion.14
  50.7 3.1 %collective-permute-done.7 = f32[4,8,1]{2,1,0:T(8,128)S(1)} collective-permute-done((f32[4,8,1]{2,1,0:T(8,128)S(1)}, f32[4,8,1]{2,1,0:T(8,128)S(1)}, u32[]{:S(2)}, u32[]{:S(2)}) %collective-permute-start.7) | collective-permute-done | bytes 160 | tf_op jit(solution)/shard_map/ppermute | solution.py:23
  53.8 0.3 fusion
  54.2 0.7 copy-done.8
  54.9 0.1 fusion.9
  55.1 1.0 fusion.11
  56.1 112.7 %all-reduce.2.cloned.1.call-done = f32[5,4096]{1,0:T(8,128)} async-done(((f32[5,4096]{1,0:T(8,128)}), f32[5,4096]{1,0:T(8,128)}) %all-reduce.2.cloned.1.call-update) | async-done | bytes 81936 | tf_op jit(solution)/shard_map/psum | solution.py:184
  168.8 0.9 slice_multiply_fusion.4
  169.8 0.7 fusion.18
  170.5 0.2 copy-done.2
  170.7 0.7 copy.19
  (64 shorter events, 1.8 us)
Async XLA Ops:
  7.2 161.7 %all-reduce.2.cloned.1.call-start = ((), (), s32[]{:S(2)}) async-start(), calls=%async_computation | async-start | bytes 262144 | tf_op jit(solution)/shard_map/psum | solution.py:184
  9.1 6.0 %copy-start.6 = (s32[4096]{0:T(1024)S(1)}, s32[4096]{0:T(1024)}, u32[]{:S(2)}) copy-start(s32[4096]{0:T(1024)} %param.15) | copy-start | bytes 49156
  9.1 6.1 %copy-start = (f32[4,8,4096]{2,1,0:T(8,128)S(1)}, f32[4,8,4096]{2,1,0:T(8,128)}, u32[]{:S(2)}) copy-start(f32[4,8,4096]{2,1,0:T(8,128)} %param.11) | copy-start | bytes 1572868
  9.2 5.9 %copy-start.1 = (f32[3,4096]{1,0:T(4,128)S(1)}, f32[3,4096]{1,0:T(4,128)}, u32[]{:S(2)}) copy-start(f32[3,4096]{1,0:T(4,128)} %param.14) | copy-start | bytes 147460
  9.2 10.3 %collective-permute-start = (f32[4,8,1]{2,1,0:T(8,128)S(1)}, f32[4,8,1]{2,1,0:T(8,128)S(1)}, u32[]{:S(2)}, u32[]{:S(2)}) collective-permute-start(f32[4,8,1]{2,1,0:T(8,128)S(1)} %get-tuple-element.55), channel_id=1, source_target_pairs={{0,1},{1,2},{2,3},{3,4},{4,5},{5,6},{6,7},{7,8},{8,9},{9,10},{10,1... | collective-permute-start | bytes 392 | tf_op jit(solution)/shard_map/ppermute | solution.py:21
  13.7 5.8 %collective-permute-start.1 = (f32[4,8,1]{2,1,0:T(8,128)S(1)}, f32[4,8,1]{2,1,0:T(8,128)S(1)}, u32[]{:S(2)}, u32[]{:S(2)}) collective-permute-start(f32[4,8,1]{2,1,0:T(8,128)S(1)} %get-tuple-element.54), channel_id=1, source_target_pairs={{1,0},{2,1},{3,2},{4,3},{5,4},{6,5},{7,6},{8,7},{9,8},{10,9},{11,1... | collective-permute-start | bytes 392 | tf_op jit(solution)/shard_map/ppermute | solution.py:23
  15.4 0.7 copy-start.13
  15.4 0.7 copy-start.14
  16.3 0.7 copy-start.10
  17.1 0.7 copy-start.9
  20.0 0.7 copy-start.3
  21.9 8.1 %collective-permute-start.2 = (f32[4,8,1]{2,1,0:T(8,128)}, f32[4,8,1]{2,1,0:T(8,128)}, u32[]{:S(2)}, u32[]{:S(2)}) collective-permute-start(f32[4,8,1]{2,1,0:T(8,128)} %get-tuple-element.50), channel_id=1, source_target_pairs={{0,1},{1,2},{2,3},{3,4},{4,5},{5,6},{6,7},{7,8},{8,9},{9,10},{10,1... | collective-permute-start | bytes 392 | tf_op jit(solution)/shard_map/ppermute | solution.py:21
  26.6 4.8 %collective-permute-start.3 = (f32[4,8,1]{2,1,0:T(8,128)}, f32[4,8,1]{2,1,0:T(8,128)}, u32[]{:S(2)}, u32[]{:S(2)}) collective-permute-start(f32[4,8,1]{2,1,0:T(8,128)} %get-tuple-element.51), channel_id=1, source_target_pairs={{1,0},{2,1},{3,2},{4,3},{5,4},{6,5},{7,6},{8,7},{9,8},{10,9},{11,1... | collective-permute-start | bytes 392 | tf_op jit(solution)/shard_map/ppermute | solution.py:23
  27.9 0.7 copy-start.12
  28.6 0.7 copy-start.11
  32.6 0.7 copy-start.4
  32.6 0.7 copy-start.7
  33.7 5.8 %collective-permute-start.4 = (f32[4,8,1]{2,1,0:T(8,128)S(1)}, f32[4,8,1]{2,1,0:T(8,128)S(1)}, u32[]{:S(2)}, u32[]{:S(2)}) collective-permute-start(f32[4,8,1]{2,1,0:T(8,128)S(1)} %get-tuple-element.46), channel_id=1, source_target_pairs={{0,1},{1,2},{2,3},{3,4},{4,5},{5,6},{6,7},{7,8},{8,9},{9,10},{10,1... | collective-permute-start | bytes 392 | tf_op jit(solution)/shard_map/ppermute | solution.py:21
  38.1 5.7 %collective-permute-start.5 = (f32[4,8,1]{2,1,0:T(8,128)S(1)}, f32[4,8,1]{2,1,0:T(8,128)S(1)}, u32[]{:S(2)}, u32[]{:S(2)}) collective-permute-start(f32[4,8,1]{2,1,0:T(8,128)S(1)} %get-tuple-element.47), channel_id=1, source_target_pairs={{1,0},{2,1},{3,2},{4,3},{5,4},{6,5},{7,6},{8,7},{9,8},{10,9},{11,1... | collective-permute-start | bytes 392 | tf_op jit(solution)/shard_map/ppermute | solution.py:23
  44.7 6.0 %collective-permute-start.6 = (f32[4,8,1]{2,1,0:T(8,128)S(1)}, f32[4,8,1]{2,1,0:T(8,128)S(1)}, u32[]{:S(2)}, u32[]{:S(2)}) collective-permute-start(f32[4,8,1]{2,1,0:T(8,128)S(1)} %get-tuple-element.42), channel_id=1, source_target_pairs={{0,1},{1,2},{2,3},{3,4},{4,5},{5,6},{6,7},{7,8},{8,9},{9,10},{10,1... | collective-permute-start | bytes 392 | tf_op jit(solution)/shard_map/ppermute | solution.py:21
  49.3 4.5 %collective-permute-start.7 = (f32[4,8,1]{2,1,0:T(8,128)S(1)}, f32[4,8,1]{2,1,0:T(8,128)S(1)}, u32[]{:S(2)}, u32[]{:S(2)}) collective-permute-start(f32[4,8,1]{2,1,0:T(8,128)S(1)} %get-tuple-element.43), channel_id=1, source_target_pairs={{1,0},{2,1},{3,2},{4,3},{5,4},{6,5},{7,6},{8,7},{9,8},{10,9},{11,1... | collective-permute-start | bytes 392 | tf_op jit(solution)/shard_map/ppermute | solution.py:23
  54.2 0.7 copy-start.8
  55.1 114.8 %copy-start.5 = (f32[4096]{0:T(1024)S(1)}, f32[4096]{0:T(1024)}, u32[]{:S(2)}) copy-start(f32[4096]{0:T(1024)} %convert_element_type.10) | copy-start | bytes 49156
  169.8 0.9 copy-start.2
Sparse Core Ops, SparseCore 0:
  30.1 138.6 all-reduce.1
where the time goes:
time: 179 us; the launch traced here: 178 us
  waiting for transfers between devices  122 us (68%)
  starting transfers between devices  23.4 us (13%)
  between operations  14.6 us (8%)
  other arithmetic  11.3 us (6%)
  local copies, waits for them, and re-layouts  7.48 us (4%)
    psum x1, waiting for transfers between devices, local(): totals = lax.psum(partial_value, 'modes')  113 us
    ppermute x4, starting transfers between devices, extended(): lax.ppermute(tail, axis, [(i, (i + 1) % count) for i in range(ends)])  18.2 us
    ppermute x4, waiting for transfers between devices, extended(): lax.ppermute(head, axis, [((i + 1) % count, i) for i in range(ends)])  8.79 us
    unnamed x31, local copies, waits for them, and re-layouts  5.75 us
    ppermute x4, starting transfers between devices, extended(): lax.ppermute(head, axis, [((i + 1) % count, i) for i in range(ends)])  5.16 us
  transfers between devices with their start and end apart: 9, of which 4 were waited for; matrix products, arithmetic and copies ran while one was open for 4% of the time, Pallas kernels for 0%

commit v1 on v0

v1 whole, which is shorter than its diff:
```python
import functools
import math

import jax
import jax.numpy as jnp
from jax import lax
from jax.experimental import pallas as pl
from jax.experimental.pallas import tpu as pltpu
from jax.sharding import PartitionSpec as P

time_step = 0.6
start_time = 10.0
exchange_coupling = 0.5
MESH = pl.DeviceIdType.MESH
LANES = 128

E4 = time_step**4 / 24.0
STAGE_WEIGHT = [
    24.0 / time_step**4,
    24.0 / time_step**3,
    12.0 / time_step**2,
    4.0 / time_step,
]


def apply_stage(y, left, right, coef, base, weight, src, masks):
    ur, dr, ui, di = y
    a_up, a_dn, fx, fy = coef
    near = [l + r for l, r in zip(left, right)]
    h_ur = a_up * ur + fx * dr + fy * di - near[0]
    h_dr = a_dn * dr + fx * ur - fy * ui - near[1]
    h_ui = a_up * ui + fx * di - fy * dr - near[2]
    h_di = a_dn * di + fx * ui + fy * ur - near[3]
    cm, sm = masks
    src_ur = cm * src[0] + sm * src[1]
    src_dr = cm * src[1] - sm * src[0]
    src_ui = cm * src[2] + sm * src[3]
    src_di = cm * src[3] - sm * src[2]
    return [
        (weight * base[0] + src_ur) + h_ui,
        (weight * base[1] + src_dr) + h_di,
        (weight * base[2] + src_ui) - h_ur,
        (weight * base[3] + src_di) - h_dr,
    ]


def kernel(
    nm,
    ns,
    sites,
    wave_hbm,
    pot_hbm,
    ang_hbm,
    mag_hbm,
    mask_hbm,
    wt_hbm,
    amp_hbm,
    grp_hbm,
    en_hbm,
    lead_hbm,
    next_out,
    dens_out,
    magn_out,
    wave,
    pot,
    ang,
    mag,
    mask,
    wt,
    amp,
    grp,
    en,
    lead,
    cos_d,
    sin_d,
    cos2_d,
    sin2_d,
    half_d,
    par,
    w,
    ya,
    yb,
    coef,
    cmask,
    edge_l,
    edge_r,
    halo_l,
    halo_r,
    part,
    slots,
    own,
    sums,
    in_sem,
    halo_send,
    halo_recv,
    rs_send,
    rs_recv,
    ag_send,
    ag_recv,
):
    chunks = sites // LANES
    share = sites // nm
    unroll = 4
    me = lax.axis_index("modes")
    tile = lax.axis_index("sites")
    left_id = lax.rem(tile + ns - 1, ns)
    right_id = lax.rem(tile + 1, ns)
    peers = [lax.rem(me + k, nm) for k in range(1, nm)]

    barrier = pltpu.get_barrier_semaphore()
    for peer in peers:
        pl.semaphore_signal(barrier, inc=1, device_id={"modes": peer}, device_id_type=MESH)
    for side in (left_id, right_id):
        pl.semaphore_signal(barrier, inc=1, device_id={"sites": side}, device_id_type=MESH)

    fetches = [
        pltpu.make_async_copy(src, dst, in_sem.at[i])
        for i, (src, dst) in enumerate(
            [
                (wt_hbm, wt),
                (amp_hbm, amp),
                (grp_hbm, grp),
                (en_hbm, en),
                (lead_hbm, lead),
                (ang_hbm, ang),
                (pot_hbm, pot),
                (mag_hbm, mag),
                (mask_hbm, mask),
                (wave_hbm, wave),
            ]
        )
    ]
    for fetch in fetches:
        fetch.start()
    for fetch in fetches[:5]:
        fetch.wait()

    group = grp[...]
    energy_row = en[...]
    energy = jnp.zeros(group.shape, jnp.float32)
    for g in range(energy_row.shape[1]):
        energy = energy + jnp.where(group == g, energy_row[:, g : g + 1], 0.0)
    amp_re = amp[0:2, :]
    amp_im = amp[2:4, :]
    rate = []
    for offset in (0.0, 0.5 * time_step, time_step):
        phase = energy * (start_time + offset)
        cosine = jnp.cos(phase)
        sine = jnp.sin(phase)
        rate.append(
            (
                amp_im * cosine - amp_re * sine,
                -(amp_re * cosine + amp_im * sine),
            )
        )
    mixes = [
        [time_step / 6.0, 4.0 * time_step / 6.0, time_step / 6.0],
        [time_step / 6.0, 2.0 * time_step / 6.0, 0.0],
        [time_step / 6.0, time_step / 6.0, 0.0],
        [time_step / 4.0, 0.0, 0.0],
    ]
    modes = group.shape[1]
    diag = lax.broadcasted_iota(jnp.int32, (modes, modes), 0) == lax.broadcasted_iota(
        jnp.int32, (modes, modes), 1
    )

    def column(row):
        spread = jnp.where(diag, jnp.broadcast_to(row, (modes, modes)), 0.0)
        return jnp.broadcast_to(jnp.sum(spread, axis=1, keepdims=True), (modes, LANES))

    for k in range(4):
        for half in range(2):
            mixed = sum(
                (STAGE_WEIGHT[k] * mixes[k][t]) * rate[t][half]
                for t in range(3)
                if mixes[k][t] != 0.0
            )
            for spin in range(2):
                par[4 * k + 2 * half + spin] = column(mixed[spin : spin + 1, :])
    par[16] = column(wt[...])
    par[17] = column(lead[...].astype(jnp.float32))

    for fetch in fetches[5:9]:
        fetch.wait()
    angle = ang[...]
    cosine = jnp.cos(angle)
    sine = jnp.sin(angle)
    cos_d[...] = cosine
    sin_d[...] = sine
    cos2_d[...] = 1.0 - 2.0 * sine * sine
    sin2_d[...] = 2.0 * sine * cosine
    half_d[...] = exchange_coupling * mask[...].astype(jnp.float32)

    zero = jnp.zeros((8, LANES), jnp.float32)
    for buf in (w, ya, yb):
        for c in range(4):
            buf[c, :, 0:LANES] = zero
            buf[c, :, LANES + sites : 2 * LANES + sites] = zero
    lane = lax.broadcasted_iota(jnp.int32, (8, LANES), 1)
    first = lane == 0
    last = lane == LANES - 1
    span = float(sites * ns // 8)

    def in_region(position):
        away = position.astype(jnp.float32) - par[17]
        return (away >= 0.0) & (away < span)

    def row(ref, i):
        return jnp.broadcast_to(ref[pl.ds(i, 1), :], (8, LANES))

    fetches[9].wait()

    def at(c, shift=0):
        return pl.ds(pl.multiple_of(c * LANES, LANES) + shift * LANES, LANES)

    def rotate(block, carry):
        for u in range(unroll):
            c = block * unroll + u
            cs = row(cos_d, c)
            sn = row(sin_d, c)
            c2 = row(cos2_d, c)
            s2 = row(sin2_d, c)
            half = row(half_d, c)
            field = [half * jnp.broadcast_to(mag[i : i + 1, at(c)], (8, LANES)) for i in range(3)]
            v = row(pot, c)
            fz = c2 * field[2] + s2 * field[0]
            coef[0, :, at(c)] = v + fz
            coef[1, :, at(c)] = v - fz
            coef[2, :, at(c)] = c2 * field[0] - s2 * field[2]
            coef[3, :, at(c)] = field[1]
            coef[4, :, at(c)] = cs
            coef[5, :, at(c)] = sn
            inside = in_region(tile * sites + c * LANES + lane)
            cmask[0, :, at(c)] = jnp.where(inside, cs, 0.0)
            cmask[1, :, at(c)] = jnp.where(inside, sn, 0.0)
            for half_i in range(2):
                up = wave[2 * half_i, :, at(c)]
                down = wave[2 * half_i + 1, :, at(c)]
                w[2 * half_i, :, at(c, 1)] = cs * up + sn * down
                w[2 * half_i + 1, :, at(c, 1)] = cs * down - sn * up
        return carry

    lax.fori_loop(0, chunks // unroll, rotate, 0)

    sub = lax.broadcasted_iota(jnp.int32, (8, LANES), 0)
    for edge, c in ((edge_l, 0), (edge_r, chunks - 1)):
        for i in range(4):
            edge[i] = w[i, :, (c + 1) * LANES : (c + 2) * LANES]
        rows = zero
        for i in range(6):
            rows = jnp.where(sub == i, coef[i, :, c * LANES : (c + 1) * LANES], rows)
        edge[4] = rows

    pl.semaphore_wait(barrier, nm + 1)
    to_left = pltpu.make_async_remote_copy(
        src_ref=edge_l,
        dst_ref=halo_r,
        send_sem=halo_send.at[0],
        recv_sem=halo_recv.at[0],
        device_id={"sites": left_id},
        device_id_type=MESH,
    )
    to_right = pltpu.make_async_remote_copy(
        src_ref=edge_r,
        dst_ref=halo_l,
        send_sem=halo_send.at[1],
        recv_sem=halo_recv.at[1],
        device_id={"sites": right_id},
        device_id_type=MESH,
    )
    to_left.start()
    to_right.start()

    all_modes = float(modes * nm)
    root = 1.0 / math.sqrt(all_modes)
    weight = par[16]

    def current(wc, wn, weight):
        after = [jnp.where(first, n, c) for c, n in zip(wc, wn)]
        after = [pltpu.roll(a, LANES - 1, 1) for a in after]
        return weight * (
            wc[0] * after[2] - wc[2] * after[0] + (wc[1] * after[3] - wc[3] * after[1])
        )

    def down_sum(x):
        return jnp.sum(x, axis=0, keepdims=True)

    def density(block, carry):
        wc = [w[i, :, at(block * unroll, 1)] for i in range(4)]
        for u in range(unroll):
            c = block * unroll + u
            wn = [w[i, :, at(c, 2)] for i in range(4)]
            ur, dr, ui, di = [wave[i, :, at(c)] for i in range(4)]
            wur, wdr, wui, wdi = [weight * x for x in (ur, dr, ui, di)]
            up = down_sum(wur * ur + wui * ui)
            dn = down_sum(wdr * dr + wdi * di)
            sx = down_sum(wur * dr + wui * di)
            sy = down_sum(wur * di - wui * dr)
            cur = down_sum(current(wc, wn, weight))
            rows = [
                (up + dn) * (1.0 / all_modes),
                sx * (2.0 * root),
                sy * (2.0 * root),
                (up - dn) * root,
                cur * (2.0 * root),
            ]
            packed = zero
            for i, r in enumerate(rows):
                packed = jnp.where(sub == i, jnp.broadcast_to(r, (8, LANES)), packed)
            part[:, at(c)] = packed
            wc = wn
        return carry

    lax.fori_loop(0, chunks // unroll, density, 0)

    scatter = []
    for k, peer in enumerate(peers):
        scatter.append(
            pltpu.make_async_remote_copy(
                src_ref=part.at[:, pl.ds(pl.multiple_of(peer * share, LANES), share)],
                dst_ref=slots.at[k],
                send_sem=rs_send,
                recv_sem=rs_recv,
                device_id={"modes": peer},
                device_id_type=MESH,
            )
        )
        scatter[-1].start()

    def stage_pass(src_ref, dst_ref, k):
        def body(block, carry):
            def load(c, shift):
                return [src_ref[i, :, at(c, shift)] for i in range(4)]

            c0 = block * unroll
            prev = load(c0, 0)
            here = load(c0, 1)
            for u in range(unroll):
                c = c0 + u
                after = load(c, 2)
                lefts = [pltpu.roll(jnp.where(last, p, h), 1, 1) for p, h in zip(prev, here)]
                rights = [
                    pltpu.roll(jnp.where(first, a, h), LANES - 1, 1) for a, h in zip(after, here)
                ]
                base = here if k == 3 else [w[i, :, at(c, 1)] for i in range(4)]
                out = apply_stage(
                    here,
                    lefts,
                    rights,
                    [coef[i, :, at(c)] for i in range(4)],
                    base,
                    STAGE_WEIGHT[k],
                    [par[4 * k + i] for i in range(4)],
                    [cmask[0, :, at(c)], cmask[1, :, at(c)]],
                )
                if k > 0:
                    for i in range(4):
                        dst_ref[i, :, at(c, 1)] = out[i]
                else:
                    cs = E4 * coef[4, :, at(c)]
                    sn = E4 * coef[5, :, at(c)]
                    for h in range(2):
                        next_out[2 * h, :, at(c)] = cs * out[2 * h] - sn * out[2 * h + 1]
                        next_out[2 * h + 1, :, at(c)] = sn * out[2 * h] + cs * out[2 * h + 1]
                prev, here = here, after
            return carry

        lax.fori_loop(0, chunks // unroll, body, 0)

    stage_pass(w, ya, 3)
    stage_pass(ya, yb, 2)
    stage_pass(yb, ya, 1)
    stage_pass(ya, None, 0)

    to_left.wait_recv()
    to_right.wait_recv()
    has_left = tile > 0
    has_right = tile < ns - 1
    base = []
    coefs = []
    masks = []
    alive = []
    for where in range(4):
        if where in (0, 3):
            halo = halo_l if where == 0 else halo_r
            there = has_left if where == 0 else has_right
            keep = jnp.full((8, LANES), there.astype(jnp.int32)) > 0
            alive.append(keep)
            base.append([jnp.where(keep, halo[i], 0.0) for i in range(4)])
            rows = [jnp.broadcast_to(halo[4, i : i + 1, :], (8, LANES)) for i in range(6)]
            coefs.append(rows[:4])
            start = tile * sites + (-LANES if where == 0 else sites)
            inside = in_region(start + lane)
            masks.append([jnp.where(inside, rows[4], 0.0), jnp.where(inside, rows[5], 0.0)])
        else:
            c = 0 if where == 1 else chunks - 1
            cut = slice(c * LANES, (c + 1) * LANES)
            alive.append(None)
            base.append([w[i, :, (c + 1) * LANES : (c + 2) * LANES] for i in range(4)])
            coefs.append([coef[i, :, cut] for i in range(4)])
            masks.append([cmask[0, :, cut], cmask[1, :, cut]])

    extra = down_sum(current(base[2], base[3], weight)) * (2.0 * root)
    extra = jnp.where(last & (sub == 5), jnp.broadcast_to(extra, (8, LANES)), 0.0)

    scatter_all = pltpu.make_async_copy(slots, slots, rs_recv)
    scatter_all.wait()
    total = part[:, pl.ds(pl.multiple_of(me * share, LANES), share)]
    for k in range(nm - 1):
        total = total + slots[k]
    own[...] = total
    own[:, share - LANES : share] = total[:, share - LANES : share] + extra
    mine = pl.ds(pl.multiple_of(me * share, LANES), share)
    gather = []
    for k, peer in enumerate(peers):
        gather.append(
            pltpu.make_async_remote_copy(
                src_ref=own,
                dst_ref=sums.at[me],
                send_sem=ag_send,
                recv_sem=ag_recv,
                device_id={"modes": peer},
                device_id_type=MESH,
            )
        )
        gather[-1].start()
    sums[me] = own[...]

    y = base
    for k in (3, 2, 1, 0):
        out = []
        for where in range(4):
            prev, here, after = y[(where + 3) % 4], y[where], y[(where + 1) % 4]
            lefts = [pltpu.roll(jnp.where(last, p, h), 1, 1) for p, h in zip(prev, here)]
            rights = [
                pltpu.roll(jnp.where(first, a, h), LANES - 1, 1) for a, h in zip(after, here)
            ]
            new = apply_stage(
                here,
                lefts,
                rights,
                coefs[where],
                base[where],
                STAGE_WEIGHT[k],
                [par[4 * k + i] for i in range(4)],
                masks[where],
            )
            if alive[where] is not None:
                new = [jnp.where(alive[where], x, 0.0) for x in new]
            out.append(new)
        y = out
    for where, c in ((1, 0), (2, chunks - 1)):
        cut = slice(c * LANES, (c + 1) * LANES)
        cs = E4 * coef[4, :, cut]
        sn = E4 * coef[5, :, cut]
        fresh = lane < 4 if where == 1 else lane >= LANES - 4
        for h in range(2):
            up = cs * y[where][2 * h] - sn * y[where][2 * h + 1]
            down = sn * y[where][2 * h] + cs * y[where][2 * h + 1]
            next_out[2 * h, :, cut] = jnp.where(fresh, up, next_out[2 * h, :, cut])
            next_out[2 * h + 1, :, cut] = jnp.where(fresh, down, next_out[2 * h + 1, :, cut])

    pltpu.make_async_copy(slots, slots, ag_recv).wait()
    bond = sums[0, :, share - LANES : share]
    for q in range(1, nm):
        bond = bond + sums[q, :, share - LANES : share]
    bond = jnp.where(last[0:1] & has_right, bond[5:6, :], 0.0)
    for q in range(nm):
        cut = slice(q * share, (q + 1) * share)
        got = sums[q]
        if q == nm - 1:
            dens_out[0:4, cut] = got[0:4, :]
            dens_out[4:5, q * share : (q + 1) * share - LANES] = got[4:5, : share - LANES]
            dens_out[4:5, (q + 1) * share - LANES : (q + 1) * share] = (
                got[4:5, share - LANES :] + bond
            )
        else:
            dens_out[:, cut] = got[0:5, :]
        turn = (time_step * exchange_coupling) * jnp.concatenate(
            [
                mask[q * share // LANES + i : q * share // LANES + i + 1, :].astype(jnp.float32)
                for i in range(share // LANES)
            ],
            axis=1,
        )
        m = [mag[i : i + 1, cut] for i in range(3)]
        hx, hy, hz = got[1:2, :], got[2:3, :], got[3:4, :]
        magn_out[0:1, cut] = m[0] - turn * (m[1] * hz - m[2] * hy)
        magn_out[1:2, cut] = m[1] - turn * (m[2] * hx - m[0] * hz)
        magn_out[2:3, cut] = m[2] - turn * (m[0] * hy - m[1] * hx)

    to_left.wait_send()
    to_right.wait_send()
    pltpu.make_async_copy(slots, slots, rs_send).wait()
    pltpu.make_async_copy(slots, slots, ag_send).wait()


def hand_out(next_v, dens_v, magn_v, next_out, dens_out, magn_out, sem):
    copies = [
        pltpu.make_async_copy(src, dst, sem.at[i])
        for i, (src, dst) in enumerate(
            [(next_v, next_out), (dens_v, dens_out), (magn_v, magn_out)]
        )
    ]
    for copy in copies:
        copy.start()
    for copy in copies:
        copy.wait()


def solution(mesh):
    nm = mesh.shape["modes"]
    ns = mesh.shape["sites"]

    def local(
        wave_state,
        potential,
        spin_angle,
        magnet,
        magnetic_mask,
        mode_weight,
        source_amp,
        mode_group,
        energies,
        lead_site,
    ):
        sites = wave_state.shape[2]
        dense = (sites // LANES, LANES)
        modes = wave_state.shape[1]
        share = sites // nm
        f32 = jnp.float32
        vmem = pltpu.VMEM
        whole = pl.BlockSpec(memory_space=pl.ANY)
        kept = pl.BlockSpec(memory_space=pltpu.VMEM)
        out = pl.pallas_call(
            functools.partial(kernel, nm, ns, sites),
            out_shape=(
                jax.ShapeDtypeStruct(wave_state.shape, f32),
                jax.ShapeDtypeStruct((5, sites), f32),
                jax.ShapeDtypeStruct((3, sites), f32),
            ),
            in_specs=[whole] * 10,
            out_specs=(kept, kept, kept),
            scratch_shapes=[
                vmem(wave_state.shape, f32),
                vmem(dense, f32),
                vmem(dense, f32),
                vmem((3, sites), f32),
                vmem(dense, jnp.int32),
                vmem((1, modes), f32),
                vmem((4, modes), f32),
                vmem((1, modes), jnp.int32),
                vmem((1, energies.shape[0]), f32),
                vmem((1, modes), jnp.int32),
                vmem(dense, f32),
                vmem(dense, f32),
                vmem(dense, f32),
                vmem(dense, f32),
                vmem(dense, f32),
                vmem((18, modes, LANES), f32),
                vmem((4, modes, sites + 2 * LANES), f32),
                vmem((4, modes, sites + 2 * LANES), f32),
                vmem((4, modes, sites + 2 * LANES), f32),
                vmem((6, modes, sites), f32),
                vmem((2, modes, sites), f32),
                vmem((5, modes, LANES), f32),
                vmem((5, modes, LANES), f32),
                vmem((5, modes, LANES), f32),
                vmem((5, modes, LANES), f32),
                vmem((8, sites), f32),
                vmem((nm - 1, 8, share), f32),
                vmem((8, share), f32),
                vmem((nm, 8, share), f32),
                pltpu.SemaphoreType.DMA((10,)),
                pltpu.SemaphoreType.DMA((2,)),
                pltpu.SemaphoreType.DMA((2,)),
                pltpu.SemaphoreType.DMA,
                pltpu.SemaphoreType.DMA,
                pltpu.SemaphoreType.DMA,
                pltpu.SemaphoreType.DMA,
            ],
            compiler_params=pltpu.CompilerParams(
                collective_id=0,
                has_side_effects=True,
                vmem_limit_bytes=32 * 1024 * 1024,
            ),
        )(
            *[
                pltpu.with_memory_space_constraint(x, pltpu.HBM)
                for x in (
                    wave_state,
                    potential.reshape(dense),
                    spin_angle.reshape(dense),
                    magnet,
                    magnetic_mask.reshape(dense),
                    mode_weight.reshape(1, modes),
                    source_amp,
                    mode_group.reshape(1, modes),
                    energies.reshape(1, -1),
                    lead_site.reshape(1, modes),
                )
            ]
        )
        return pl.pallas_call(
            hand_out,
            out_shape=tuple(jax.ShapeDtypeStruct(x.shape, f32) for x in out),
            in_specs=[kept] * 3,
            out_specs=(whole,) * 3,
            scratch_shapes=[pltpu.SemaphoreType.DMA((3,))],
            compiler_params=pltpu.CompilerParams(vmem_limit_bytes=2 * 1024 * 1024),
        )(*out)

    return jax.shard_map(
        local,
        mesh=mesh,
        in_specs=(
            P(None, "modes", "sites"),
            P("sites"),
            P("sites"),
            P(None, "sites"),
            P("sites"),
            P("modes"),
            P(None, "modes"),
            P("modes"),
            P(),
            P("modes"),
        ),
        out_specs=(P(None, "modes", "sites"), P(None, "sites"), P(None, "sites")),
        check_vma=False,
    )
```

time: 179 us -> 26.1 us (0.15)
  waiting for transfers between devices: 122 us -> 0 us
  Pallas kernels: 0 us -> 25.3 us
  starting transfers between devices: 23.4 us -> 0 us
  between operations: 14.6 us -> 0.64 us
  other arithmetic: 11.3 us -> 0 us
  local copies, waits for them, and re-layouts: 7.48 us -> 0 us
    psum x1 -> x0, waiting for transfers between devices: 113 us -> none  [local(): totals = lax.psum(partial_value, 'modes')]
    pallas_call x0 -> x2, Pallas kernels: none -> 25.3 us  [the longest x1 24.5 us: local(): pl.pallas_call(functools.partial(kernel, nm, ns, sites), out_shape=(jax.S...]
    ppermute x8 -> x0, starting transfers between devices: 23.3 us -> none  [the longest x4 18.2 us: extended(): lax.ppermute(tail, axis, [(i, (i + 1) % count) for i in range(ends)])]
    ppermute x8 -> x0, waiting for transfers between devices: 8.8 us -> none  [the longest x4 8.79 us: extended(): lax.ppermute(head, axis, [((i + 1) % count, i) for i in range(ends)])]
    unnamed x31 -> x0, local copies, waits for them, and re-layouts: 5.75 us -> none
    add x22 -> x0, other arithmetic: 5.2 us -> none  [the longest x3 1.75 us: rate(): left_w + right_w]
  transfers between devices with their start and end apart: 9 -> 0, of which waited for: 4 -> 0; matrix products, arithmetic and copies ran while one was open for 4% -> 0% of each run, Pallas kernels for 0% -> 0%
where the time goes in v1:
time: 26.1 us; the launch traced here: 26 us
  Pallas kernels  25.3 us (97%)
  between operations  0.64 us (2%)
    pallas_call x1, Pallas kernels, local(): pl.pallas_call(functools.partial(kernel, nm, ns, sites), out_shape=(jax.S...  24.5 us
    pallas_call x1, Pallas kernels, local(): pl.pallas_call(hand_out, out_shape=tuple((jax.ShapeDtypeStruct(x.shape, f...  0.87 us

profile of v1, /device:TPU:1, one launch (start us, length us, event | category | flops | bytes accessed | tf_op | source)
XLA Modules:
  0.0 26.0 jit_solution(16853088989182478958)
XLA Ops:
  0.6 24.5 %shard_map.121 = (f32[4,8,4096]{2,1,0:T(8,128)S(1)}, f32[5,4096]{1,0:T(8,128)S(1)}, f32[3,4096]{1,0:T(4,128)S(1)}) custom-call(f32[4,8,4096]{2,1,0:T(8,128)} %wave_hbm.1, f32[32,128]{1,0:T(8,128)} %bitcast.7, f32[32,128]{1,0:T(8,128)} %bitcast.8, f32[3,4096]{1,0:T(4,128)} %mag_hbm.1, s32[32,128]{1,0:T(8,128)} %bitcast.9, f32[1,8]{1,0:T(1,128)} %bitcast.10, ...), custom_call_target="tpu_custom_call" | custom-call | tf_op jit(solution)/shard_map/pallas_call | solution.py:535
  25.1 0.9 %shard_map.122 = (f32[4,8,4096]{2,1,0:T(8,128)}, f32[5,4096]{1,0:T(8,128)}, f32[3,4096]{1,0:T(4,128)}) custom-call(f32[4,8,4096]{2,1,0:T(8,128)S(1)} %get-tuple-element.6.next_v, f32[5,4096]{1,0:T(8,128)S(1)} %get-tuple-element.7.dens_v, f32[3,4096]{1,0:T(4,128)S(1)} %get-tuple-element.8.magn_v), custom_call_target="tpu_custom_call" | custom-call | tf_op jit(solution)/shard_map/pallas_call | solution.py:604

commit v2 on v1

--- a/solution.py
+++ b/solution.py
@@ -13,6 +13,7 @@
 exchange_coupling = 0.5
 MESH = pl.DeviceIdType.MESH
 LANES = 128
+OWNERS = 4
 
 E4 = time_step**4 / 24.0
 STAGE_WEIGHT = [
@@ -76,6 +77,8 @@
     cos2_d,
     sin2_d,
     half_d,
+    mag_d,
+    mag_n,
     par,
     w,
     ya,
@@ -86,6 +89,10 @@
     edge_r,
     halo_l,
     halo_r,
+    bond_a,
+    bond_b,
+    slots_a,
+    slots_b,
     part,
     slots,
     own,
@@ -93,25 +100,64 @@
     in_sem,
     halo_send,
     halo_recv,
+    a_send,
+    a_recv,
+    b_send,
+    b_recv,
     rs_send,
     rs_recv,
     ag_send,
     ag_recv,
+    ready,
 ):
     chunks = sites // LANES
-    share = sites // nm
+    owners = min(OWNERS, nm)
+    run = chunks // owners
     unroll = 4
     me = lax.axis_index("modes")
     tile = lax.axis_index("sites")
-    left_id = lax.rem(tile + ns - 1, ns)
-    right_id = lax.rem(tile + 1, ns)
-    peers = [lax.rem(me + k, nm) for k in range(1, nm)]
+    turn_tile = ns // 2
+    has_left = tile > 0
+    has_right = tile < ns - 1
+    is_owner = me < owners
+    keeper = owners - 1
+    keeps = me == keeper
+    early = tile == turn_tile
+    late = tile == turn_tile - 1
+    order = [k for k in (1, 2, 3, 4, 5, 6, 7, 12, 13, 14, 15, 8, 9, 10, 11) if k < nm]
+
+    def signal(sem, where):
+        pl.semaphore_signal(sem, inc=1, device_id=where, device_id_type=MESH)
+
+    def send(src, dst, send_sem, recv_sem, where):
+        return pltpu.make_async_remote_copy(
+            src_ref=src,
+            dst_ref=dst,
+            send_sem=send_sem,
+            recv_sem=recv_sem,
+            device_id=where,
+            device_id_type=MESH,
+        )
 
     barrier = pltpu.get_barrier_semaphore()
-    for peer in peers:
-        pl.semaphore_signal(barrier, inc=1, device_id={"modes": peer}, device_id_type=MESH)
-    for side in (left_id, right_id):
-        pl.semaphore_signal(barrier, inc=1, device_id={"sites": side}, device_id_type=MESH)
+
+    @pl.when(is_owner)
+    def _():
+        for k in order:
+            signal(barrier, {"modes": me ^ k})
+
+    @pl.when(has_right & jnp.logical_not(late))
+    def _():
+        signal(barrier, {"sites": tile + 1})
+
+    @pl.when(early)
+    def _():
+        signal(barrier, {"sites": tile - 1})
+
+    @pl.when(keeps & has_right & jnp.logical_not(late))
+    def _():
+        for m in range(nm):
+            signal(barrier, {"modes": jnp.int32(m), "sites": tile + 1})
 
     fetches = [
         pltpu.make_async_copy(src, dst, in_sem.at[i])
@@ -130,7 +176,7 @@
             ]
         )
     ]
-    for fetch in fetches:
+    for fetch in reversed(fetches):
         fetch.start()
     for fetch in fetches[:5]:
         fetch.wait()
@@ -197,6 +243,7 @@
             buf[c, :, 0:LANES] = zero
             buf[c, :, LANES + sites : 2 * LANES + sites] = zero
     lane = lax.broadcasted_iota(jnp.int32, (8, LANES), 1)
+    sub = lax.broadcasted_iota(jnp.int32, (8, LANES), 0)
     first = lane == 0
     last = lane == LANES - 1
     span = float(sites * ns // 8)
@@ -233,16 +280,19 @@
             inside = in_region(tile * sites + c * LANES + lane)
             cmask[0, :, at(c)] = jnp.where(inside, cs, 0.0)
             cmask[1, :, at(c)] = jnp.where(inside, sn, 0.0)
-            for half_i in range(2):
-                up = wave[2 * half_i, :, at(c)]
-                down = wave[2 * half_i + 1, :, at(c)]
-                w[2 * half_i, :, at(c, 1)] = cs * up + sn * down
-                w[2 * half_i + 1, :, at(c, 1)] = cs * down - sn * up
+            for part_i in range(2):
+                up = wave[2 * part_i, :, at(c)]
+                down = wave[2 * part_i + 1, :, at(c)]
+                w[2 * part_i, :, at(c, 1)] = cs * up + sn * down
+                w[2 * part_i + 1, :, at(c, 1)] = cs * down - sn * up
         return carry
 
     lax.fori_loop(0, chunks // unroll, rotate, 0)
 
-    sub = lax.broadcasted_iota(jnp.int32, (8, LANES), 0)
+    all_modes = float(modes * nm)
+    root = 1.0 / math.sqrt(all_modes)
+    weight = par[16]
+
     for edge, c in ((edge_l, 0), (edge_r, chunks - 1)):
         for i in range(4):
             edge[i] = w[i, :, (c + 1) * LANES : (c + 2) * LANES]
@@ -250,30 +300,52 @@
         for i in range(6):
             rows = jnp.where(sub == i, coef[i, :, c * LANES : (c + 1) * LANES], rows)
         edge[4] = rows
-
-    pl.semaphore_wait(barrier, nm + 1)
-    to_left = pltpu.make_async_remote_copy(
-        src_ref=edge_l,
-        dst_ref=halo_r,
-        send_sem=halo_send.at[0],
-        recv_sem=halo_recv.at[0],
-        device_id={"sites": left_id},
-        device_id_type=MESH,
+    left_factor = zero
+    right_factor = zero
+    for i in range(4):
+        left_factor = jnp.where(lane == i, pltpu.roll(edge_r[i], 1 + i, 1), left_factor)
+        other = edge_l[(i + 2) % 4]
+        other = pltpu.roll(other, i, 1) if i else other
+        right_factor = jnp.where(lane == i, other if i < 2 else -other, right_factor)
+    bond_a[...] = (2.0 * root) * (weight * left_factor)
+    bond_b[...] = right_factor
+
+    to_left = send(
+        edge_l, halo_r, halo_send.at[0], halo_recv.at[0], {"sites": jnp.maximum(tile - 1, 0)}
     )
-    to_right = pltpu.make_async_remote_copy(
-        src_ref=edge_r,
-        dst_ref=halo_l,
-        send_sem=halo_send.at[1],
-        recv_sem=halo_recv.at[1],
-        device_id={"sites": right_id},
-        device_id_type=MESH,
+    to_right = send(
+        edge_r, halo_l, halo_send.at[1], halo_recv.at[1], {"sites": jnp.minimum(tile + 1, ns - 1)}
     )
-    to_left.start()
-    to_right.start()
-
-    all_modes = float(modes * nm)
-    root = 1.0 / math.sqrt(all_modes)
-    weight = par[16]
+    to_keeper = send(bond_a, slots_a.at[me], a_send, a_recv, {"modes": jnp.int32(keeper)})
+    to_left_keeper = send(
+        bond_b,
+        slots_b.at[me],
+        b_send,
+        b_recv,
+        {"modes": jnp.int32(keeper), "sites": jnp.maximum(tile - 1, 0)},
+    )
+
+    pl.semaphore_wait(
+        barrier,
+        owners
+        - is_owner.astype(jnp.int32)
+        + 2 * (has_left & jnp.logical_not(early)).astype(jnp.int32)
+        + late.astype(jnp.int32),
+    )
+
+    @pl.when(late)
+    def _():
+        signal(ready, {"sites": tile + 1})
+        to_right.start()
+
+    @pl.when(has_left & jnp.logical_not(early))
+    def _():
+        to_left_keeper.start()
+        to_left.start()
+
+    @pl.when(jnp.logical_not(keeps))
+    def _():
+        to_keeper.start()
 
     def current(wc, wn, weight):
         after = [jnp.where(first, n, c) for c, n in zip(wc, wn)]
@@ -285,10 +357,14 @@
     def down_sum(x):
         return jnp.sum(x, axis=0, keepdims=True)
 
+    run_sub = lax.broadcasted_iota(jnp.int32, (run, LANES), 0)
+
     def density(block, carry):
-        wc = [w[i, :, at(block * unroll, 1)] for i in range(4)]
-        for u in range(unroll):
-            c = block * unroll + u
+        q = lax.rem(block + me, owners)
+        wc = [w[i, :, at(q * run, 1)] for i in range(4)]
+        packed = [jnp.zeros((run, LANES), jnp.float32) for _ in range(5)]
+        for u in range(run):
+            c = q * run + u
             wn = [w[i, :, at(c, 2)] for i in range(4)]
             ur, dr, ui, di = [wave[i, :, at(c)] for i in range(4)]
             wur, wdr, wui, wdi = [weight * x for x in (ur, dr, ui, di)]
@@ -297,35 +373,27 @@
             sx = down_sum(wur * dr + wui * di)
             sy = down_sum(wur * di - wui * dr)
             cur = down_sum(current(wc, wn, weight))
-            rows = [
-                (up + dn) * (1.0 / all_modes),
-                sx * (2.0 * root),
-                sy * (2.0 * root),
-                (up - dn) * root,
-                cur * (2.0 * root),
-            ]
-            packed = zero
-            for i, r in enumerate(rows):
-                packed = jnp.where(sub == i, jnp.broadcast_to(r, (8, LANES)), packed)
-            part[:, at(c)] = packed
+            for i, r in enumerate([up, sx, sy, dn, cur]):
+                packed[i] = jnp.where(run_sub == u, jnp.broadcast_to(r, (run, LANES)), packed[i])
             wc = wn
+        up, sx, sy, dn, cur = packed
+        rows = [
+            (up + dn) * (1.0 / all_modes),
+            sx * (2.0 * root),
+            sy * (2.0 * root),
+            (up - dn) * root,
+            cur * (2.0 * root),
+        ]
+        for i, r in enumerate(rows):
+            part[q, i * run : (i + 1) * run, :] = r
+
+        @pl.when(q != me)
+        def _():
+            send(part.at[q], slots.at[me], rs_send.at[q], rs_recv, {"modes": q}).start()
+
         return carry
 
-    lax.fori_loop(0, chunks // unroll, density, 0)
-
-    scatter = []
-    for k, peer in enumerate(peers):
-        scatter.append(
-            pltpu.make_async_remote_copy(
-                src_ref=part.at[:, pl.ds(pl.multiple_of(peer * share, LANES), share)],
-                dst_ref=slots.at[k],
-                send_sem=rs_send,
-                recv_sem=rs_recv,
-                device_id={"modes": peer},
-                device_id_type=MESH,
-            )
-        )
-        scatter[-1].start()
+    lax.fori_loop(0, owners, density, 0)
 
     def stage_pass(src_ref, dst_ref, k):
         def body(block, carry):
@@ -370,129 +438,168 @@
     stage_pass(w, ya, 3)
     stage_pass(ya, yb, 2)
     stage_pass(yb, ya, 1)
+
+    @pl.when(has_right & jnp.logical_not(late))
+    def _():
+        to_left.wait_recv()
+        to_right.start()
+
+    @pl.when(is_owner)
+    def _():
+        pltpu.make_async_copy(
+            slots.at[0 : nm - 1], slots.at[0 : nm - 1], rs_recv
+        ).wait()
+        total = part[me]
+        for k in range(1, nm):
+            total = total + slots[me ^ k]
+        own[...] = total
+
+        @pl.when(keeps)
+        def _():
+            pltpu.make_async_copy(
+                slots_a.at[0 : nm - 1], slots_a.at[0 : nm - 1], a_recv
+            ).wait()
+
+        @pl.when(keeps & has_right)
+        def _():
+            pltpu.make_async_copy(slots_b, slots_b, b_recv).wait()
+            bond = bond_a[...] * slots_b[keeper]
+            for m in range(nm):
+                if m != keeper:
+                    bond = bond + slots_a[m] * slots_b[m]
+            bond = jnp.sum(down_sum(bond), axis=1, keepdims=True)
+            spot = (run_sub[0:1] == 0) & last[0:1]
+            end = 5 * run - 1
+            own[end : end + 1, :] = own[end : end + 1, :] + jnp.where(
+                spot, jnp.broadcast_to(bond, (1, LANES)), 0.0
+            )
+
+        for k in order:
+            send(own, sums.at[me], ag_send, ag_recv.at[me], {"modes": me ^ k}).start()
+        sums[me] = own[...]
+
     stage_pass(ya, None, 0)
-
-    to_left.wait_recv()
-    to_right.wait_recv()
-    has_left = tile > 0
-    has_right = tile < ns - 1
-    base = []
-    coefs = []
-    masks = []
-    alive = []
-    for where in range(4):
-        if where in (0, 3):
-            halo = halo_l if where == 0 else halo_r
-            there = has_left if where == 0 else has_right
-            keep = jnp.full((8, LANES), there.astype(jnp.int32)) > 0
-            alive.append(keep)
-            base.append([jnp.where(keep, halo[i], 0.0) for i in range(4)])
-            rows = [jnp.broadcast_to(halo[4, i : i + 1, :], (8, LANES)) for i in range(6)]
-            coefs.append(rows[:4])
-            start = tile * sites + (-LANES if where == 0 else sites)
-            inside = in_region(start + lane)
-            masks.append([jnp.where(inside, rows[4], 0.0), jnp.where(inside, rows[5], 0.0)])
-        else:
-            c = 0 if where == 1 else chunks - 1
+    for i in range(3):
+        for c in range(chunks):
+            mag_d[i, c : c + 1, :] = mag[i : i + 1, c * LANES : (c + 1) * LANES]
+
+    def redo_ends():
+        @pl.when(has_left)
+        def _():
+            to_right.wait_recv()
+
+        @pl.when(late)
+        def _():
+            to_left.wait_recv()
+
+        base = []
+        coefs = []
+        masks = []
+        alive = []
+        for where in range(4):
+            if where in (0, 3):
+                halo = halo_l if where == 0 else halo_r
+                there = has_left if where == 0 else has_right
+                keep = jnp.full((8, LANES), there.astype(jnp.int32)) > 0
+                alive.append(keep)
+                base.append([jnp.where(keep, halo[i], 0.0) for i in range(4)])
+                rows = [jnp.broadcast_to(halo[4, i : i + 1, :], (8, LANES)) for i in range(6)]
+                coefs.append(rows[:4])
+                start = tile * sites + (-LANES if where == 0 else sites)
+                inside = in_region(start + lane)
+                masks.append([jnp.where(inside, rows[4], 0.0), jnp.where(inside, rows[5], 0.0)])
+            else:
+                c = 0 if where == 1 else chunks - 1
+                cut = slice(c * LANES, (c + 1) * LANES)
+                alive.append(None)
+                base.append([w[i, :, (c + 1) * LANES : (c + 2) * LANES] for i in range(4)])
+                coefs.append([coef[i, :, cut] for i in range(4)])
+                masks.append([cmask[0, :, cut], cmask[1, :, cut]])
+        y = base
+        for k in (3, 2, 1, 0):
+            out = []
+            for where in range(4):
+                prev, here, after = y[(where + 3) % 4], y[where], y[(where + 1) % 4]
+                lefts = [pltpu.roll(jnp.where(last, p, h), 1, 1) for p, h in zip(prev, here)]
+                rights = [
+                    pltpu.roll(jnp.where(first, a, h), LANES - 1, 1) for a, h in zip(after, here)
+                ]
+                new = apply_stage(
+                    here,
+                    lefts,
+                    rights,
+                    coefs[where],
+                    base[where],
+                    STAGE_WEIGHT[k],
+                    [par[4 * k + i] for i in range(4)],
+                    masks[where],
+                )
+                if alive[where] is not None:
+                    new = [jnp.where(alive[where], x, 0.0) for x in new]
+                out.append(new)
+            y = out
+        for where, c in ((1, 0), (2, chunks - 1)):
             cut = slice(c * LANES, (c + 1) * LANES)
-            alive.append(None)
-            base.append([w[i, :, (c + 1) * LANES : (c + 2) * LANES] for i in range(4)])
-            coefs.append([coef[i, :, cut] for i in range(4)])
-            masks.append([cmask[0, :, cut], cmask[1, :, cut]])
-
-    extra = down_sum(current(base[2], base[3], weight)) * (2.0 * root)
-    extra = jnp.where(last & (sub == 5), jnp.broadcast_to(extra, (8, LANES)), 0.0)
-
-    scatter_all = pltpu.make_async_copy(slots, slots, rs_recv)
-    scatter_all.wait()
-    total = part[:, pl.ds(pl.multiple_of(me * share, LANES), share)]
-    for k in range(nm - 1):
-        total = total + slots[k]
-    own[...] = total
-    own[:, share - LANES : share] = total[:, share - LANES : share] + extra
-    mine = pl.ds(pl.multiple_of(me * share, LANES), share)
-    gather = []
-    for k, peer in enumerate(peers):
-        gather.append(
-            pltpu.make_async_remote_copy(
-                src_ref=own,
-                dst_ref=sums.at[me],
-                send_sem=ag_send,
-                recv_sem=ag_recv,
-                device_id={"modes": peer},
-                device_id_type=MESH,
-            )
-        )
-        gather[-1].start()
-    sums[me] = own[...]
-
-    y = base
-    for k in (3, 2, 1, 0):
-        out = []
-        for where in range(4):
-            prev, here, after = y[(where + 3) % 4], y[where], y[(where + 1) % 4]
-            lefts = [pltpu.roll(jnp.where(last, p, h), 1, 1) for p, h in zip(prev, here)]
-            rights = [
-                pltpu.roll(jnp.where(first, a, h), LANES - 1, 1) for a, h in zip(after, here)
-            ]
-            new = apply_stage(
-                here,
-                lefts,
-                rights,
-                coefs[where],
-                base[where],
-                STAGE_WEIGHT[k],
-                [par[4 * k + i] for i in range(4)],
-                masks[where],
-            )
-            if alive[where] is not None:
-                new = [jnp.where(alive[where], x, 0.0) for x in new]
-            out.append(new)
-        y = out
-    for where, c in ((1, 0), (2, chunks - 1)):
-        cut = slice(c * LANES, (c + 1) * LANES)
-        cs = E4 * coef[4, :, cut]
-        sn = E4 * coef[5, :, cut]
-        fresh = lane < 4 if where == 1 else lane >= LANES - 4
-        for h in range(2):
-            up = cs * y[where][2 * h] - sn * y[where][2 * h + 1]
-            down = sn * y[where][2 * h] + cs * y[where][2 * h + 1]
-            next_out[2 * h, :, cut] = jnp.where(fresh, up, next_out[2 * h, :, cut])
-            next_out[2 * h + 1, :, cut] = jnp.where(fresh, down, next_out[2 * h + 1, :, cut])
-
-    pltpu.make_async_copy(slots, slots, ag_recv).wait()
-    bond = sums[0, :, share - LANES : share]
-    for q in range(1, nm):
-        bond = bond + sums[q, :, share - LANES : share]
-    bond = jnp.where(last[0:1] & has_right, bond[5:6, :], 0.0)
-    for q in range(nm):
-        cut = slice(q * share, (q + 1) * share)
-        got = sums[q]
-        if q == nm - 1:
-            dens_out[0:4, cut] = got[0:4, :]
-            dens_out[4:5, q * share : (q + 1) * share - LANES] = got[4:5, : share - LANES]
-            dens_out[4:5, (q + 1) * share - LANES : (q + 1) * share] = (
-                got[4:5, share - LANES :] + bond
-            )
-        else:
-            dens_out[:, cut] = got[0:5, :]
-        turn = (time_step * exchange_coupling) * jnp.concatenate(
-            [
-                mask[q * share // LANES + i : q * share // LANES + i + 1, :].astype(jnp.float32)
-                for i in range(share // LANES)
-            ],
-            axis=1,
-        )
-        m = [mag[i : i + 1, cut] for i in range(3)]
-        hx, hy, hz = got[1:2, :], got[2:3, :], got[3:4, :]
-        magn_out[0:1, cut] = m[0] - turn * (m[1] * hz - m[2] * hy)
-        magn_out[1:2, cut] = m[1] - turn * (m[2] * hx - m[0] * hz)
-        magn_out[2:3, cut] = m[2] - turn * (m[0] * hy - m[1] * hx)
-
-    to_left.wait_send()
-    to_right.wait_send()
-    pltpu.make_async_copy(slots, slots, rs_send).wait()
-    pltpu.make_async_copy(slots, slots, ag_send).wait()
+            cs = E4 * coef[4, :, cut]
+            sn = E4 * coef[5, :, cut]
+            fresh = lane < 4 if where == 1 else lane >= LANES - 4
+            for h in range(2):
+                up = cs * y[where][2 * h] - sn * y[where][2 * h + 1]
+                down = sn * y[where][2 * h] + cs * y[where][2 * h + 1]
+                next_out[2 * h, :, cut] = jnp.where(fresh, up, next_out[2 * h, :, cut])
+                next_out[2 * h + 1, :, cut] = jnp.where(fresh, down, next_out[2 * h + 1, :, cut])
+
+    @pl.when(jnp.logical_not(early))
+    def _():
+        redo_ends()
+
+    @pl.when(early)
+    def _():
+        pl.semaphore_wait(ready, 1)
+        to_left_keeper.start()
+        to_left.start()
+
+    for q in range(owners):
+        @pl.when(me != q)
+        def _():
+            pltpu.make_async_copy(own, sums.at[q], ag_recv.at[q]).wait()
+
+        hx, hy, hz = [sums[q, i * run : (i + 1) * run, :] for i in (1, 2, 3)]
+        m = [mag_d[i, q * run : (q + 1) * run, :] for i in range(3)]
+        turn = time_step * half_d[q * run : (q + 1) * run, :]
+        mag_n[0:run, :] = m[0] - turn * (m[1] * hz - m[2] * hy)
+        mag_n[run : 2 * run, :] = m[1] - turn * (m[2] * hx - m[0] * hz)
+        mag_n[2 * run : 3 * run, :] = m[2] - turn * (m[0] * hy - m[1] * hx)
+        for u in range(run):
+            cut = slice((q * run + u) * LANES, (q * run + u + 1) * LANES)
+            dens_out[:, cut] = sums[q, pl.ds(u, 5, stride=run), :]
+            magn_out[:, cut] = mag_n[pl.ds(u, 3, stride=run), :]
+
+    @pl.when(early)
+    def _():
+        redo_ends()
+
+    @pl.when(has_right)
+    def _():
+        to_right.wait_send()
+
+    @pl.when(has_left)
+    def _():
+        to_left.wait_send()
+        to_left_keeper.wait_send()
+
+    @pl.when(jnp.logical_not(keeps))
+    def _():
+        to_keeper.wait_send()
+
+    for q in range(owners):
+        @pl.when(me != q)
+        def _():
+            pltpu.make_async_copy(own, own, rs_send.at[q]).wait()
+
+    @pl.when(is_owner)
+    def _():
+        pltpu.make_async_copy(slots.at[0 : nm - 1], slots.at[0 : nm - 1], ag_send).wait()
 
 
 def hand_out(next_v, dens_v, magn_v, next_out, dens_out, magn_out, sem):
@@ -527,7 +634,8 @@
         sites = wave_state.shape[2]
         dense = (sites // LANES, LANES)
         modes = wave_state.shape[1]
-        share = sites // nm
+        owners = min(OWNERS, nm)
+        rows = 5 * dense[0] // owners
         f32 = jnp.float32
         vmem = pltpu.VMEM
         whole = pl.BlockSpec(memory_space=pl.ANY)
@@ -557,6 +665,8 @@
                 vmem(dense, f32),
                 vmem(dense, f32),
                 vmem(dense, f32),
+                vmem((3, *dense), f32),
+                vmem((3 * rows // 5, LANES), f32),
                 vmem((18, modes, LANES), f32),
                 vmem((4, modes, sites + 2 * LANES), f32),
                 vmem((4, modes, sites + 2 * LANES), f32),
@@ -567,10 +677,14 @@
                 vmem((5, modes, LANES), f32),
                 vmem((5, modes, LANES), f32),
                 vmem((5, modes, LANES), f32),
-                vmem((8, sites), f32),
-                vmem((nm - 1, 8, share), f32),
-                vmem((8, share), f32),
-                vmem((nm, 8, share), f32),
+                vmem((modes, LANES), f32),
+                vmem((modes, LANES), f32),
+                vmem((nm, modes, LANES), f32),
+                vmem((nm, modes, LANES), f32),
+                vmem((owners, rows, LANES), f32),
+                vmem((nm, rows, LANES), f32),
+                vmem((rows, LANES), f32),
+                vmem((owners, rows, LANES), f32),
                 pltpu.SemaphoreType.DMA((10,)),
                 pltpu.SemaphoreType.DMA((2,)),
                 pltpu.SemaphoreType.DMA((2,)),
@@ -578,6 +692,11 @@
                 pltpu.SemaphoreType.DMA,
                 pltpu.SemaphoreType.DMA,
                 pltpu.SemaphoreType.DMA,
+                pltpu.SemaphoreType.DMA((owners,)),
+                pltpu.SemaphoreType.DMA,
+                pltpu.SemaphoreType.DMA,
+                pltpu.SemaphoreType.DMA((owners,)),
+                pltpu.SemaphoreType.REGULAR,
             ],
             compiler_params=pltpu.CompilerParams(
                 collective_id=0,

time: 26.1 us -> 22 us (0.84)
  the two profiles are of different devices: /device:TPU:1 before, /device:TPU:17 now
where the time goes in v2:
time: 22 us; the launch traced here: 21.8 us
  Pallas kernels  21.2 us (96%)
  between operations  0.64 us (3%)
    pallas_call x1, Pallas kernels, local(): pl.pallas_call(functools.partial(kernel, nm, ns, sites), out_shape=(jax.S...  20.3 us
    pallas_call x1, Pallas kernels, local(): pl.pallas_call(hand_out, out_shape=tuple((jax.ShapeDtypeStruct(x.shape, f...  0.87 us

profile of v2, /device:TPU:17, one launch (start us, length us, event | category | flops | bytes accessed | tf_op | source)
XLA Modules:
  0.0 21.8 jit_solution(2459964961543253365)
XLA Ops:
  0.6 20.3 %shard_map.121 = (f32[4,8,4096]{2,1,0:T(8,128)S(1)}, f32[5,4096]{1,0:T(8,128)S(1)}, f32[3,4096]{1,0:T(4,128)S(1)}) custom-call(f32[4,8,4096]{2,1,0:T(8,128)} %wave_hbm.1, f32[32,128]{1,0:T(8,128)} %bitcast.7, f32[32,128]{1,0:T(8,128)} %bitcast.8, f32[3,4096]{1,0:T(4,128)} %mag_hbm.1, s32[32,128]{1,0:T(8,128)} %bitcast.9, f32[1,8]{1,0:T(1,128)} %bitcast.10, ...), custom_call_target="tpu_custom_call" | custom-call | tf_op jit(solution)/shard_map/pallas_call | solution.py:643
  21.0 0.9 %shard_map.122 = (f32[4,8,4096]{2,1,0:T(8,128)}, f32[5,4096]{1,0:T(8,128)}, f32[3,4096]{1,0:T(4,128)}) custom-call(f32[4,8,4096]{2,1,0:T(8,128)S(1)} %get-tuple-element.6.next_v, f32[5,4096]{1,0:T(8,128)S(1)} %get-tuple-element.7.dens_v, f32[3,4096]{1,0:T(4,128)S(1)} %get-tuple-element.8.magn_v), custom_call_target="tpu_custom_call" | custom-call | tf_op jit(solution)/shard_map/pallas_call | solution.py:723

commit v3 on v2

--- a/solution.py
+++ b/solution.py
@@ -13,7 +13,8 @@
 exchange_coupling = 0.5
 MESH = pl.DeviceIdType.MESH
 LANES = 128
-OWNERS = 4
+SHARES = 8
+FIRST_TILE_OWNERS = {16: (1, 1, 2, 3, 4, 5, 12, 13), 4: (1, 1, 1, 1, 2, 2, 3, 3)}
 
 E4 = time_step**4 / 24.0
 STAGE_WEIGHT = [
@@ -95,9 +96,9 @@
     slots_b,
     part,
     slots,
-    own,
     sums,
     in_sem,
+    wave_sem,
     halo_send,
     halo_recv,
     a_send,
@@ -111,20 +112,39 @@
     ready,
 ):
     chunks = sites // LANES
-    owners = min(OWNERS, nm)
-    run = chunks // owners
+    run = chunks // SHARES
     unroll = 4
     me = lax.axis_index("modes")
     tile = lax.axis_index("sites")
     turn_tile = ns // 2
     has_left = tile > 0
     has_right = tile < ns - 1
-    is_owner = me < owners
-    keeper = owners - 1
-    keeps = me == keeper
     early = tile == turn_tile
     late = tile == turn_tile - 1
-    order = [k for k in (1, 2, 3, 4, 5, 6, 7, 12, 13, 14, 15, 8, 9, 10, 11) if k < nm]
+    usual = [q * min(nm, SHARES) // SHARES for q in range(SHARES)]
+    special = FIRST_TILE_OWNERS.get(nm, usual)
+
+    def owner_of(q):
+        return jnp.where(tile == 0, jnp.int32(special[q]), jnp.int32(usual[q]))
+
+    def owner_at(q):
+        found = owner_of(0)
+        for i in range(1, SHARES):
+            found = jnp.where(q == i, owner_of(i), found)
+        return found
+
+    def among(devices):
+        found = me == devices[0]
+        for d in devices[1:]:
+            found = found | (me == d)
+        return found
+
+    is_owner = jnp.where(tile == 0, among(sorted(set(special))).astype(jnp.int32), among(sorted(set(usual))).astype(jnp.int32))
+    owner_count = jnp.where(tile == 0, len(set(special)), len(set(usual)))
+    keeper = owner_of(SHARES - 1)
+    keeps = me == keeper
+    left_keeper = jnp.where(tile == 1, jnp.int32(special[-1]), jnp.int32(usual[-1]))
+    order = [j for j in (1, 3, 0, 2, 5, 7, 4, 6, 9, 11, 8, 10, 13, 15, 12, 14) if j < nm]
 
     def signal(sem, where):
         pl.semaphore_signal(sem, inc=1, device_id=where, device_id_type=MESH)
@@ -141,9 +161,9 @@
 
     barrier = pltpu.get_barrier_semaphore()
 
-    @pl.when(is_owner)
-    def _():
-        for k in order:
+    @pl.when(is_owner == 1)
+    def _():
+        for k in range(1, nm):
             signal(barrier, {"modes": me ^ k})
 
     @pl.when(has_right & jnp.logical_not(late))
@@ -172,12 +192,20 @@
                 (pot_hbm, pot),
                 (mag_hbm, mag),
                 (mask_hbm, mask),
-                (wave_hbm, wave),
             ]
         )
     ]
-    for fetch in reversed(fetches):
+
+    def piece(q):
+        cut = pl.ds(pl.multiple_of(q * (run * LANES), LANES), run * LANES)
+        return pltpu.make_async_copy(
+            wave_hbm.at[:, :, cut], wave.at[:, :, cut], wave_sem.at[q]
+        )
+
+    for fetch in fetches:
         fetch.start()
+    for q in (0, SHARES - 1, *range(1, SHARES - 1)):
+        piece(q).start()
     for fetch in fetches[:5]:
         fetch.wait()
 
@@ -255,14 +283,13 @@
     def row(ref, i):
         return jnp.broadcast_to(ref[pl.ds(i, 1), :], (8, LANES))
 
-    fetches[9].wait()
-
     def at(c, shift=0):
         return pl.ds(pl.multiple_of(c * LANES, LANES) + shift * LANES, LANES)
 
-    def rotate(block, carry):
-        for u in range(unroll):
-            c = block * unroll + u
+    def rotate(q):
+        piece(q).wait()
+        for u in range(run):
+            c = q * run + u
             cs = row(cos_d, c)
             sn = row(sin_d, c)
             c2 = row(cos2_d, c)
@@ -285,13 +312,25 @@
                 down = wave[2 * part_i + 1, :, at(c)]
                 w[2 * part_i, :, at(c, 1)] = cs * up + sn * down
                 w[2 * part_i + 1, :, at(c, 1)] = cs * down - sn * up
-        return carry
-
-    lax.fori_loop(0, chunks // unroll, rotate, 0)
+
+    pl.semaphore_wait(
+        barrier,
+        owner_count
+        - is_owner
+        + 2 * (has_left & jnp.logical_not(early)).astype(jnp.int32)
+        + late.astype(jnp.int32),
+    )
+
+    @pl.when(late)
+    def _():
+        signal(ready, {"sites": tile + 1})
+
+    rotate(0)
+    rotate(SHARES - 1)
 
     all_modes = float(modes * nm)
     root = 1.0 / math.sqrt(all_modes)
-    weight = par[16]
+    weight = root * par[16]
 
     for edge, c in ((edge_l, 0), (edge_r, chunks - 1)):
         for i in range(4):
@@ -307,7 +346,7 @@
         other = edge_l[(i + 2) % 4]
         other = pltpu.roll(other, i, 1) if i else other
         right_factor = jnp.where(lane == i, other if i < 2 else -other, right_factor)
-    bond_a[...] = (2.0 * root) * (weight * left_factor)
+    bond_a[...] = 2.0 * (weight * left_factor)
     bond_b[...] = right_factor
 
     to_left = send(
@@ -316,26 +355,17 @@
     to_right = send(
         edge_r, halo_l, halo_send.at[1], halo_recv.at[1], {"sites": jnp.minimum(tile + 1, ns - 1)}
     )
-    to_keeper = send(bond_a, slots_a.at[me], a_send, a_recv, {"modes": jnp.int32(keeper)})
+    to_keeper = send(bond_a, slots_a.at[me], a_send, a_recv, {"modes": keeper})
     to_left_keeper = send(
         bond_b,
         slots_b.at[me],
         b_send,
         b_recv,
-        {"modes": jnp.int32(keeper), "sites": jnp.maximum(tile - 1, 0)},
+        {"modes": left_keeper, "sites": jnp.maximum(tile - 1, 0)},
     )
 
-    pl.semaphore_wait(
-        barrier,
-        owners
-        - is_owner.astype(jnp.int32)
-        + 2 * (has_left & jnp.logical_not(early)).astype(jnp.int32)
-        + late.astype(jnp.int32),
-    )
-
     @pl.when(late)
     def _():
-        signal(ready, {"sites": tile + 1})
         to_right.start()
 
     @pl.when(has_left & jnp.logical_not(early))
@@ -357,43 +387,59 @@
     def down_sum(x):
         return jnp.sum(x, axis=0, keepdims=True)
 
-    run_sub = lax.broadcasted_iota(jnp.int32, (run, LANES), 0)
-
-    def density(block, carry):
-        q = lax.rem(block + me, owners)
+    odd = (sub & 1) == 1
+    upper_pair = (sub & 2) == 2
+    lower_half = sub < 4
+
+    def fold(x, y, other, shift):
+        return jnp.where(other, y, x) + pltpu.roll(jnp.where(other, x, y), 8 - shift, 0)
+
+    def fold_four(x):
+        return fold(fold(x[0], x[1], odd, 1), fold(x[2], x[3], odd, 1), upper_pair, 2)
+
+    def fold_eight(x):
+        return fold(fold_four(x[:4]), fold_four(x[4:]), jnp.logical_not(lower_half), 4)
+
+    first_scale = jnp.where(lower_half, root, 2.0)
+    second_scale = jnp.where(lower_half, 2.0, 1.0)
+
+    def density(q):
         wc = [w[i, :, at(q * run, 1)] for i in range(4)]
-        packed = [jnp.zeros((run, LANES), jnp.float32) for _ in range(5)]
+        tiles = [[], [], [], [], []]
         for u in range(run):
             c = q * run + u
             wn = [w[i, :, at(c, 2)] for i in range(4)]
             ur, dr, ui, di = [wave[i, :, at(c)] for i in range(4)]
             wur, wdr, wui, wdi = [weight * x for x in (ur, dr, ui, di)]
-            up = down_sum(wur * ur + wui * ui)
-            dn = down_sum(wdr * dr + wdi * di)
-            sx = down_sum(wur * dr + wui * di)
-            sy = down_sum(wur * di - wui * dr)
-            cur = down_sum(current(wc, wn, weight))
-            for i, r in enumerate([up, sx, sy, dn, cur]):
-                packed[i] = jnp.where(run_sub == u, jnp.broadcast_to(r, (run, LANES)), packed[i])
+            up = wur * ur + wui * ui
+            dn = wdr * dr + wdi * di
+            tiles[0].append(up + dn)
+            tiles[1].append(wur * dr + wui * di)
+            tiles[2].append(wur * di - wui * dr)
+            tiles[3].append(up - dn)
+            tiles[4].append(current(wc, wn, weight))
             wc = wn
-        up, sx, sy, dn, cur = packed
-        rows = [
-            (up + dn) * (1.0 / all_modes),
-            sx * (2.0 * root),
-            sy * (2.0 * root),
-            (up - dn) * root,
-            cur * (2.0 * root),
-        ]
-        for i, r in enumerate(rows):
-            part[q, i * run : (i + 1) * run, :] = r
-
-        @pl.when(q != me)
+        part[q, 0:8, :] = first_scale * fold_eight(tiles[0] + tiles[1])
+        part[q, 8:16, :] = second_scale * fold_eight(tiles[2] + tiles[3])
+        bonds = fold_four(tiles[4])
+        part[q, 16:20, :] = (2.0 * (bonds + pltpu.roll(bonds, 4, 0)))[0:4, :]
+        owner = owner_at(q)
+
+        @pl.when(owner != me)
         def _():
-            send(part.at[q], slots.at[me], rs_send.at[q], rs_recv, {"modes": q}).start()
-
+            send(part.at[q], slots.at[q, me], rs_send.at[q], rs_recv.at[q], {"modes": owner}).start()
+
+    def stream(q, carry):
+        rotate(q)
+        density(q - 1)
         return carry
 
-    lax.fori_loop(0, owners, density, 0)
+    def finish(q, carry):
+        density(q)
+        return carry
+
+    lax.fori_loop(1, SHARES - 1, stream, 0)
+    lax.fori_loop(SHARES - 2, SHARES, finish, 0)
 
     def stage_pass(src_ref, dst_ref, k):
         def body(block, carry):
@@ -444,39 +490,49 @@
         to_left.wait_recv()
         to_right.start()
 
-    @pl.when(is_owner)
-    def _():
-        pltpu.make_async_copy(
-            slots.at[0 : nm - 1], slots.at[0 : nm - 1], rs_recv
-        ).wait()
-        total = part[me]
-        for k in range(1, nm):
-            total = total + slots[me ^ k]
-        own[...] = total
-
-        @pl.when(keeps)
+    def add_up(q, carry):
+        @pl.when(owner_at(q) == me)
         def _():
             pltpu.make_async_copy(
-                slots_a.at[0 : nm - 1], slots_a.at[0 : nm - 1], a_recv
+                slots.at[q, 0 : nm - 1], slots.at[q, 0 : nm - 1], rs_recv.at[q]
             ).wait()
-
-        @pl.when(keeps & has_right)
-        def _():
-            pltpu.make_async_copy(slots_b, slots_b, b_recv).wait()
-            bond = bond_a[...] * slots_b[keeper]
-            for m in range(nm):
-                if m != keeper:
-                    bond = bond + slots_a[m] * slots_b[m]
-            bond = jnp.sum(down_sum(bond), axis=1, keepdims=True)
-            spot = (run_sub[0:1] == 0) & last[0:1]
-            end = 5 * run - 1
-            own[end : end + 1, :] = own[end : end + 1, :] + jnp.where(
-                spot, jnp.broadcast_to(bond, (1, LANES)), 0.0
-            )
-
-        for k in order:
-            send(own, sums.at[me], ag_send, ag_recv.at[me], {"modes": me ^ k}).start()
-        sums[me] = own[...]
+            total = part[q]
+            for k in range(1, nm):
+                total = total + slots[q, me ^ k]
+            sums[q] = total
+
+            @pl.when(q == SHARES - 1)
+            def _():
+                pltpu.make_async_copy(
+                    slots_a.at[0 : nm - 1], slots_a.at[0 : nm - 1], a_recv
+                ).wait()
+
+            @pl.when((q == SHARES - 1) & has_right)
+            def _():
+                pltpu.make_async_copy(slots_b, slots_b, b_recv).wait()
+                bond = bond_a[...] * slots_b[me]
+                for k in range(1, nm):
+                    bond = bond + slots_a[me ^ k] * slots_b[me ^ k]
+                bond = jnp.sum(down_sum(bond), axis=1, keepdims=True)
+                end = 5 * run - 1
+                sums[q, end : end + 1, :] = sums[q, end : end + 1, :] + jnp.where(
+                    last[0:1], jnp.broadcast_to(bond, (1, LANES)), 0.0
+                )
+
+            for j in order:
+                @pl.when(me != j)
+                def _():
+                    send(
+                        sums.at[q],
+                        sums.at[q],
+                        ag_send.at[q],
+                        ag_recv.at[q],
+                        {"modes": jnp.int32(j)},
+                    ).start()
+
+        return carry
+
+    lax.fori_loop(0, SHARES, add_up, 0)
 
     stage_pass(ya, None, 0)
     for i in range(3):
@@ -559,10 +615,10 @@
         to_left_keeper.start()
         to_left.start()
 
-    for q in range(owners):
-        @pl.when(me != q)
+    for q in range(SHARES):
+        @pl.when(owner_of(q) != me)
         def _():
-            pltpu.make_async_copy(own, sums.at[q], ag_recv.at[q]).wait()
+            pltpu.make_async_copy(sums.at[q], sums.at[q], ag_recv.at[q]).wait()
 
         hx, hy, hz = [sums[q, i * run : (i + 1) * run, :] for i in (1, 2, 3)]
         m = [mag_d[i, q * run : (q + 1) * run, :] for i in range(3)]
@@ -592,14 +648,20 @@
     def _():
         to_keeper.wait_send()
 
-    for q in range(owners):
-        @pl.when(me != q)
+    def settle(q, carry):
+        @pl.when(owner_at(q) != me)
         def _():
-            pltpu.make_async_copy(own, own, rs_send.at[q]).wait()
-
-    @pl.when(is_owner)
-    def _():
-        pltpu.make_async_copy(slots.at[0 : nm - 1], slots.at[0 : nm - 1], ag_send).wait()
+            pltpu.make_async_copy(part.at[q], part.at[q], rs_send.at[q]).wait()
+
+        @pl.when(owner_at(q) == me)
+        def _():
+            pltpu.make_async_copy(
+                slots.at[q, 0 : nm - 1], slots.at[q, 0 : nm - 1], ag_send.at[q]
+            ).wait()
+
+        return carry
+
+    lax.fori_loop(0, SHARES, settle, 0)
 
 
 def hand_out(next_v, dens_v, magn_v, next_out, dens_out, magn_out, sem):
@@ -634,8 +696,7 @@
         sites = wave_state.shape[2]
         dense = (sites // LANES, LANES)
         modes = wave_state.shape[1]
-        owners = min(OWNERS, nm)
-        rows = 5 * dense[0] // owners
+        rows = 5 * dense[0] // SHARES
         f32 = jnp.float32
         vmem = pltpu.VMEM
         whole = pl.BlockSpec(memory_space=pl.ANY)
@@ -681,21 +742,21 @@
                 vmem((modes, LANES), f32),
                 vmem((nm, modes, LANES), f32),
                 vmem((nm, modes, LANES), f32),
-                vmem((owners, rows, LANES), f32),
-                vmem((nm, rows, LANES), f32),
-                vmem((rows, LANES), f32),
-                vmem((owners, rows, LANES), f32),
-                pltpu.SemaphoreType.DMA((10,)),
+                vmem((SHARES, rows, LANES), f32),
+                vmem((SHARES, nm, rows, LANES), f32),
+                vmem((SHARES, rows, LANES), f32),
+                pltpu.SemaphoreType.DMA((9,)),
+                pltpu.SemaphoreType.DMA((SHARES,)),
                 pltpu.SemaphoreType.DMA((2,)),
                 pltpu.SemaphoreType.DMA((2,)),
                 pltpu.SemaphoreType.DMA,
                 pltpu.SemaphoreType.DMA,
                 pltpu.SemaphoreType.DMA,
                 pltpu.SemaphoreType.DMA,
-                pltpu.SemaphoreType.DMA((owners,)),
-                pltpu.SemaphoreType.DMA,
-                pltpu.SemaphoreType.DMA,
-                pltpu.SemaphoreType.DMA((owners,)),
+                pltpu.SemaphoreType.DMA((SHARES,)),
+                pltpu.SemaphoreType.DMA((SHARES,)),
+                pltpu.SemaphoreType.DMA((SHARES,)),
+                pltpu.SemaphoreType.DMA((SHARES,)),
                 pltpu.SemaphoreType.REGULAR,
             ],
             compiler_params=pltpu.CompilerParams(

time: 22 us -> 18.2 us (0.83)
  the two profiles are of different devices: /device:TPU:17 before, /device:TPU:1 now
where the time goes in v3:
time: 18.2 us; the launch traced here: 18.1 us
  Pallas kernels  17.4 us (96%)
  between operations  0.64 us (4%)
    pallas_call x1, Pallas kernels, local(): pl.pallas_call(functools.partial(kernel, nm, ns, sites), out_shape=(jax.S...  16.5 us
    pallas_call x1, Pallas kernels, local(): pl.pallas_call(hand_out, out_shape=tuple((jax.ShapeDtypeStruct(x.shape, f...  0.87 us

profile of v3, /device:TPU:1, one launch (start us, length us, event | category | flops | bytes accessed | tf_op | source)
XLA Modules:
  0.0 18.1 jit_solution(2667961612939225965)
XLA Ops:
  0.6 16.5 %shard_map.121 = (f32[4,8,4096]{2,1,0:T(8,128)S(1)}, f32[5,4096]{1,0:T(8,128)S(1)}, f32[3,4096]{1,0:T(4,128)S(1)}) custom-call(f32[4,8,4096]{2,1,0:T(8,128)} %wave_hbm.1, f32[32,128]{1,0:T(8,128)} %bitcast.7, f32[32,128]{1,0:T(8,128)} %bitcast.8, f32[3,4096]{1,0:T(4,128)} %mag_hbm.1, s32[32,128]{1,0:T(8,128)} %bitcast.9, f32[1,8]{1,0:T(1,128)} %bitcast.10, ...), custom_call_target="tpu_custom_call" | custom-call | tf_op jit(solution)/shard_map/pallas_call | solution.py:704
  17.2 0.9 %shard_map.122 = (f32[4,8,4096]{2,1,0:T(8,128)}, f32[5,4096]{1,0:T(8,128)}, f32[3,4096]{1,0:T(4,128)}) custom-call(f32[4,8,4096]{2,1,0:T(8,128)S(1)} %get-tuple-element.6.next_v, f32[5,4096]{1,0:T(8,128)S(1)} %get-tuple-element.7.dens_v, f32[3,4096]{1,0:T(4,128)S(1)} %get-tuple-element.8.magn_v), custom_call_target="tpu_custom_call" | custom-call | tf_op jit(solution)/shard_map/pallas_call | solution.py:784

commit v4 on v3

--- a/solution.py
+++ b/solution.py
@@ -14,7 +14,7 @@
 MESH = pl.DeviceIdType.MESH
 LANES = 128
 SHARES = 8
-FIRST_TILE_OWNERS = {16: (1, 1, 2, 3, 4, 5, 12, 13), 4: (1, 1, 1, 1, 2, 2, 3, 3)}
+FIRST_TILE_OWNERS = {16: (1, 1, 1, 1, 2, 3, 4, 5), 4: (1, 1, 1, 1, 2, 2, 3, 3)}
 
 E4 = time_step**4 / 24.0
 STAGE_WEIGHT = [
@@ -119,8 +119,10 @@
     turn_tile = ns // 2
     has_left = tile > 0
     has_right = tile < ns - 1
-    early = tile == turn_tile
-    late = tile == turn_tile - 1
+    at_turn = tile == turn_tile
+    before_turn = tile == turn_tile - 1
+    early = at_turn | ((tile == 1) & (me == 0))
+    late = before_turn | ((tile == 0) & (me == 0))
     usual = [q * min(nm, SHARES) // SHARES for q in range(SHARES)]
     special = FIRST_TILE_OWNERS.get(nm, usual)
 
@@ -144,7 +146,7 @@
     keeper = owner_of(SHARES - 1)
     keeps = me == keeper
     left_keeper = jnp.where(tile == 1, jnp.int32(special[-1]), jnp.int32(usual[-1]))
-    order = [j for j in (1, 3, 0, 2, 5, 7, 4, 6, 9, 11, 8, 10, 13, 15, 12, 14) if j < nm]
+    order = [j for j in (1, 3, 0, 2, 5, 7, 4, 6, 13, 15, 12, 14, 9, 11, 8, 10) if j < nm]
 
     def signal(sem, where):
         pl.semaphore_signal(sem, inc=1, device_id=where, device_id_type=MESH)
@@ -174,7 +176,7 @@
     def _():
         signal(barrier, {"sites": tile - 1})
 
-    @pl.when(keeps & has_right & jnp.logical_not(late))
+    @pl.when(keeps & has_right & jnp.logical_not(before_turn))
     def _():
         for m in range(nm):
             signal(barrier, {"modes": jnp.int32(m), "sites": tile + 1})
@@ -206,6 +208,19 @@
         fetch.start()
     for q in (0, SHARES - 1, *range(1, SHARES - 1)):
         piece(q).start()
+    pl.semaphore_wait(
+        barrier,
+        owner_count
+        - is_owner
+        + (has_left & jnp.logical_not(early)).astype(jnp.int32)
+        + (has_left & jnp.logical_not(at_turn)).astype(jnp.int32)
+        + late.astype(jnp.int32),
+    )
+
+    @pl.when(late)
+    def _():
+        signal(ready, {"sites": tile + 1})
+
     for fetch in fetches[:5]:
         fetch.wait()
 
@@ -286,45 +301,39 @@
     def at(c, shift=0):
         return pl.ds(pl.multiple_of(c * LANES, LANES) + shift * LANES, LANES)
 
+    def site_terms(c):
+        cs = row(cos_d, c)
+        sn = row(sin_d, c)
+        c2 = row(cos2_d, c)
+        s2 = row(sin2_d, c)
+        half = row(half_d, c)
+        field = [half * jnp.broadcast_to(mag[i : i + 1, at(c)], (8, LANES)) for i in range(3)]
+        v = row(pot, c)
+        fz = c2 * field[2] + s2 * field[0]
+        coef[0, :, at(c)] = v + fz
+        coef[1, :, at(c)] = v - fz
+        coef[2, :, at(c)] = c2 * field[0] - s2 * field[2]
+        coef[3, :, at(c)] = field[1]
+        coef[4, :, at(c)] = cs
+        coef[5, :, at(c)] = sn
+        inside = in_region(tile * sites + c * LANES + lane)
+        cmask[0, :, at(c)] = jnp.where(inside, cs, 0.0)
+        cmask[1, :, at(c)] = jnp.where(inside, sn, 0.0)
+
     def rotate(q):
         piece(q).wait()
         for u in range(run):
             c = q * run + u
             cs = row(cos_d, c)
             sn = row(sin_d, c)
-            c2 = row(cos2_d, c)
-            s2 = row(sin2_d, c)
-            half = row(half_d, c)
-            field = [half * jnp.broadcast_to(mag[i : i + 1, at(c)], (8, LANES)) for i in range(3)]
-            v = row(pot, c)
-            fz = c2 * field[2] + s2 * field[0]
-            coef[0, :, at(c)] = v + fz
-            coef[1, :, at(c)] = v - fz
-            coef[2, :, at(c)] = c2 * field[0] - s2 * field[2]
-            coef[3, :, at(c)] = field[1]
-            coef[4, :, at(c)] = cs
-            coef[5, :, at(c)] = sn
-            inside = in_region(tile * sites + c * LANES + lane)
-            cmask[0, :, at(c)] = jnp.where(inside, cs, 0.0)
-            cmask[1, :, at(c)] = jnp.where(inside, sn, 0.0)
             for part_i in range(2):
                 up = wave[2 * part_i, :, at(c)]
                 down = wave[2 * part_i + 1, :, at(c)]
                 w[2 * part_i, :, at(c, 1)] = cs * up + sn * down
                 w[2 * part_i + 1, :, at(c, 1)] = cs * down - sn * up
 
-    pl.semaphore_wait(
-        barrier,
-        owner_count
-        - is_owner
-        + 2 * (has_left & jnp.logical_not(early)).astype(jnp.int32)
-        + late.astype(jnp.int32),
-    )
-
-    @pl.when(late)
-    def _():
-        signal(ready, {"sites": tile + 1})
-
+    site_terms(0)
+    site_terms(chunks - 1)
     rotate(0)
     rotate(SHARES - 1)
 
@@ -368,9 +377,12 @@
     def _():
         to_right.start()
 
+    @pl.when(has_left & jnp.logical_not(at_turn))
+    def _():
+        to_left_keeper.start()
+
     @pl.when(has_left & jnp.logical_not(early))
     def _():
-        to_left_keeper.start()
         to_left.start()
 
     @pl.when(jnp.logical_not(keeps))
@@ -481,6 +493,12 @@
 
         lax.fori_loop(0, chunks // unroll, body, 0)
 
+    def terms(block, carry):
+        for u in range(unroll):
+            site_terms(block * unroll + u)
+        return carry
+
+    lax.fori_loop(0, chunks // unroll, terms, 0)
     stage_pass(w, ya, 3)
     stage_pass(ya, yb, 2)
     stage_pass(yb, ya, 1)
@@ -491,14 +509,17 @@
         to_right.start()
 
     def add_up(q, carry):
-        @pl.when(owner_at(q) == me)
+        owns = owner_at(q) == me
+
+        @pl.when(owns)
         def _():
+            slots[q, me] = part[q]
             pltpu.make_async_copy(
                 slots.at[q, 0 : nm - 1], slots.at[q, 0 : nm - 1], rs_recv.at[q]
             ).wait()
-            total = part[q]
-            for k in range(1, nm):
-                total = total + slots[q, me ^ k]
+            total = slots[q, 0]
+            for d in range(1, nm):
+                total = total + slots[q, d]
             sums[q] = total
 
             @pl.when(q == SHARES - 1)
@@ -612,8 +633,11 @@
     @pl.when(early)
     def _():
         pl.semaphore_wait(ready, 1)
+        to_left.start()
+
+    @pl.when(at_turn)
+    def _():
         to_left_keeper.start()
-        to_left.start()
 
     for q in range(SHARES):
         @pl.when(owner_of(q) != me)

time: 18.2 us -> 17.6 us (0.967)
  the two profiles are of different devices: /device:TPU:1 before, /device:TPU:4 now
where the time goes in v4:
time: 17.6 us; the launch traced here: 17.4 us
  Pallas kernels  16.8 us (95%)
  between operations  0.64 us (4%)
    pallas_call x1, Pallas kernels, local(): pl.pallas_call(functools.partial(kernel, nm, ns, sites), out_shape=(jax.S...  15.9 us
    pallas_call x1, Pallas kernels, local(): pl.pallas_call(hand_out, out_shape=tuple((jax.ShapeDtypeStruct(x.shape, f...  0.87 us

profile of v4, /device:TPU:4, one launch (start us, length us, event | category | flops | bytes accessed | tf_op | source)
XLA Modules:
  0.0 17.4 jit_solution(12404720542869338075)
XLA Ops:
  0.6 15.9 %shard_map.121 = (f32[4,8,4096]{2,1,0:T(8,128)S(1)}, f32[5,4096]{1,0:T(8,128)S(1)}, f32[3,4096]{1,0:T(4,128)S(1)}) custom-call(f32[4,8,4096]{2,1,0:T(8,128)} %wave_hbm.1, f32[32,128]{1,0:T(8,128)} %bitcast.7, f32[32,128]{1,0:T(8,128)} %bitcast.8, f32[3,4096]{1,0:T(4,128)} %mag_hbm.1, s32[32,128]{1,0:T(8,128)} %bitcast.9, f32[1,8]{1,0:T(1,128)} %bitcast.10, ...), custom_call_target="tpu_custom_call" | custom-call | tf_op jit(solution)/shard_map/pallas_call | solution.py:728
  16.6 0.9 %shard_map.122 = (f32[4,8,4096]{2,1,0:T(8,128)}, f32[5,4096]{1,0:T(8,128)}, f32[3,4096]{1,0:T(4,128)}) custom-call(f32[4,8,4096]{2,1,0:T(8,128)S(1)} %get-tuple-element.6.next_v, f32[5,4096]{1,0:T(8,128)S(1)} %get-tuple-element.7.dens_v, f32[3,4096]{1,0:T(4,128)S(1)} %get-tuple-element.8.magn_v), custom_call_target="tpu_custom_call" | custom-call | tf_op jit(solution)/shard_map/pallas_call | solution.py:808

commit v5 on v4

--- a/solution.py
+++ b/solution.py
@@ -121,9 +121,10 @@
     has_right = tile < ns - 1
     at_turn = tile == turn_tile
     before_turn = tile == turn_tile - 1
-    early = at_turn | ((tile == 1) & (me == 0))
-    late = before_turn | ((tile == 0) & (me == 0))
+    early = at_turn | before_turn | ((tile == 1) & (me == 0))
+    late = before_turn | (tile == turn_tile - 2) | ((tile == 0) & (me == 0))
     usual = [q * min(nm, SHARES) // SHARES for q in range(SHARES)]
+    usual = [1, 3, 5, 7, 1, 3, 5, 7] if nm == 16 else usual
     special = FIRST_TILE_OWNERS.get(nm, usual)
 
     def owner_of(q):
@@ -176,7 +177,7 @@
     def _():
         signal(barrier, {"sites": tile - 1})
 
-    @pl.when(keeps & has_right & jnp.logical_not(before_turn))
+    @pl.when(keeps & has_right & (tile != turn_tile - 2) & jnp.logical_not(before_turn))
     def _():
         for m in range(nm):
             signal(barrier, {"modes": jnp.int32(m), "sites": tile + 1})
@@ -213,7 +214,7 @@
         owner_count
         - is_owner
         + (has_left & jnp.logical_not(early)).astype(jnp.int32)
-        + (has_left & jnp.logical_not(at_turn)).astype(jnp.int32)
+        + (has_left & jnp.logical_not(at_turn | before_turn)).astype(jnp.int32)
         + late.astype(jnp.int32),
     )
 
@@ -341,18 +342,23 @@
     root = 1.0 / math.sqrt(all_modes)
     weight = root * par[16]
 
-    for edge, c in ((edge_l, 0), (edge_r, chunks - 1)):
-        for i in range(4):
-            edge[i] = w[i, :, (c + 1) * LANES : (c + 2) * LANES]
+    ends = []
+    for edge, c, back in ((edge_r, chunks - 1, 4), (edge_l, 0, 0)):
         rows = zero
         for i in range(6):
             rows = jnp.where(sub == i, coef[i, :, c * LANES : (c + 1) * LANES], rows)
-        edge[4] = rows
+        packed = pltpu.roll(rows, 16 + back, 1)
+        state = [w[i, :, (c + 1) * LANES : (c + 2) * LANES] for i in range(4)]
+        for i in range(4):
+            moved = pltpu.roll(state[i], 4 * i + back, 1) if i or back else state[i]
+            packed = jnp.where((lane >= 4 * i) & (lane < 4 * i + 4), moved, packed)
+        edge[...] = packed
+        ends.append(state)
     left_factor = zero
     right_factor = zero
     for i in range(4):
-        left_factor = jnp.where(lane == i, pltpu.roll(edge_r[i], 1 + i, 1), left_factor)
-        other = edge_l[(i + 2) % 4]
+        left_factor = jnp.where(lane == i, pltpu.roll(ends[0][i], 1 + i, 1), left_factor)
+        other = ends[1][(i + 2) % 4]
         other = pltpu.roll(other, i, 1) if i else other
         right_factor = jnp.where(lane == i, other if i < 2 else -other, right_factor)
     bond_a[...] = 2.0 * (weight * left_factor)
@@ -377,7 +383,7 @@
     def _():
         to_right.start()
 
-    @pl.when(has_left & jnp.logical_not(at_turn))
+    @pl.when(has_left & jnp.logical_not(at_turn | before_turn))
     def _():
         to_left_keeper.start()
 
@@ -452,6 +458,12 @@
 
     lax.fori_loop(1, SHARES - 1, stream, 0)
     lax.fori_loop(SHARES - 2, SHARES, finish, 0)
+
+    @pl.when(before_turn)
+    def _():
+        pl.semaphore_wait(ready, 1)
+        to_left_keeper.start()
+        to_left.start()
 
     def stage_pass(src_ref, dst_ref, k):
         def body(block, carry):
@@ -579,8 +591,15 @@
                 there = has_left if where == 0 else has_right
                 keep = jnp.full((8, LANES), there.astype(jnp.int32)) > 0
                 alive.append(keep)
-                base.append([jnp.where(keep, halo[i], 0.0) for i in range(4)])
-                rows = [jnp.broadcast_to(halo[4, i : i + 1, :], (8, LANES)) for i in range(6)]
+                back = 4 if where == 0 else 0
+                packed = halo[...]
+                state = [
+                    pltpu.roll(packed, LANES - 4 * i - back, 1) if i or back else packed
+                    for i in range(4)
+                ]
+                base.append([jnp.where(keep, x, 0.0) for x in state])
+                rows = pltpu.roll(packed, LANES - 16 - back, 1)
+                rows = [jnp.broadcast_to(rows[i : i + 1, :], (8, LANES)) for i in range(6)]
                 coefs.append(rows[:4])
                 start = tile * sites + (-LANES if where == 0 else sites)
                 inside = in_region(start + lane)
@@ -630,14 +649,17 @@
     def _():
         redo_ends()
 
-    @pl.when(early)
+    @pl.when(early & jnp.logical_not(before_turn))
     def _():
         pl.semaphore_wait(ready, 1)
+
+    @pl.when(at_turn)
+    def _():
+        to_left_keeper.start()
+
+    @pl.when(early & jnp.logical_not(before_turn))
+    def _():
         to_left.start()
-
-    @pl.when(at_turn)
-    def _():
-        to_left_keeper.start()
 
     for q in range(SHARES):
         @pl.when(owner_of(q) != me)
@@ -758,10 +780,10 @@
                 vmem((4, modes, sites + 2 * LANES), f32),
                 vmem((6, modes, sites), f32),
                 vmem((2, modes, sites), f32),
-                vmem((5, modes, LANES), f32),
-                vmem((5, modes, LANES), f32),
-                vmem((5, modes, LANES), f32),
-                vmem((5, modes, LANES), f32),
+                vmem((modes, LANES), f32),
+                vmem((modes, LANES), f32),
+                vmem((modes, LANES), f32),
+                vmem((modes, LANES), f32),
                 vmem((modes, LANES), f32),
                 vmem((modes, LANES), f32),
                 vmem((nm, modes, LANES), f32),

time: 17.6 us -> 17.1 us (0.972)
  the two profiles are of different devices: /device:TPU:4 before, /device:TPU:1 now
where the time goes in v5:
time: 17.1 us; the launch traced here: 16.9 us
  Pallas kernels  16.3 us (95%)
  between operations  0.64 us (4%)
    pallas_call x1, Pallas kernels, local(): pl.pallas_call(functools.partial(kernel, nm, ns, sites), out_shape=(jax.S...  15.4 us
    pallas_call x1, Pallas kernels, local(): pl.pallas_call(hand_out, out_shape=tuple((jax.ShapeDtypeStruct(x.shape, f...  0.87 us

profile of v5, /device:TPU:1, one launch (start us, length us, event | category | flops | bytes accessed | tf_op | source)
XLA Modules:
  0.0 16.9 jit_solution(15417035370767467657)
XLA Ops:
  0.6 15.4 %shard_map.121 = (f32[4,8,4096]{2,1,0:T(8,128)S(1)}, f32[5,4096]{1,0:T(8,128)S(1)}, f32[3,4096]{1,0:T(4,128)S(1)}) custom-call(f32[4,8,4096]{2,1,0:T(8,128)} %wave_hbm.1, f32[32,128]{1,0:T(8,128)} %bitcast.7, f32[32,128]{1,0:T(8,128)} %bitcast.8, f32[3,4096]{1,0:T(4,128)} %mag_hbm.1, s32[32,128]{1,0:T(8,128)} %bitcast.9, f32[1,8]{1,0:T(1,128)} %bitcast.10, ...), custom_call_target="tpu_custom_call" | custom-call | tf_op jit(solution)/shard_map/pallas_call | solution.py:750
  16.0 0.9 %shard_map.122 = (f32[4,8,4096]{2,1,0:T(8,128)}, f32[5,4096]{1,0:T(8,128)}, f32[3,4096]{1,0:T(4,128)}) custom-call(f32[4,8,4096]{2,1,0:T(8,128)S(1)} %get-tuple-element.6.next_v, f32[5,4096]{1,0:T(8,128)S(1)} %get-tuple-element.7.dens_v, f32[3,4096]{1,0:T(4,128)S(1)} %get-tuple-element.8.magn_v), custom_call_target="tpu_custom_call" | custom-call | tf_op jit(solution)/shard_map/pallas_call | solution.py:830

commit v6 on v5

--- a/solution.py
+++ b/solution.py
@@ -225,31 +225,7 @@
     for fetch in fetches[:5]:
         fetch.wait()
 
-    group = grp[...]
-    energy_row = en[...]
-    energy = jnp.zeros(group.shape, jnp.float32)
-    for g in range(energy_row.shape[1]):
-        energy = energy + jnp.where(group == g, energy_row[:, g : g + 1], 0.0)
-    amp_re = amp[0:2, :]
-    amp_im = amp[2:4, :]
-    rate = []
-    for offset in (0.0, 0.5 * time_step, time_step):
-        phase = energy * (start_time + offset)
-        cosine = jnp.cos(phase)
-        sine = jnp.sin(phase)
-        rate.append(
-            (
-                amp_im * cosine - amp_re * sine,
-                -(amp_re * cosine + amp_im * sine),
-            )
-        )
-    mixes = [
-        [time_step / 6.0, 4.0 * time_step / 6.0, time_step / 6.0],
-        [time_step / 6.0, 2.0 * time_step / 6.0, 0.0],
-        [time_step / 6.0, time_step / 6.0, 0.0],
-        [time_step / 4.0, 0.0, 0.0],
-    ]
-    modes = group.shape[1]
+    modes = wt.shape[1]
     diag = lax.broadcasted_iota(jnp.int32, (modes, modes), 0) == lax.broadcasted_iota(
         jnp.int32, (modes, modes), 1
     )
@@ -258,15 +234,6 @@
         spread = jnp.where(diag, jnp.broadcast_to(row, (modes, modes)), 0.0)
         return jnp.broadcast_to(jnp.sum(spread, axis=1, keepdims=True), (modes, LANES))
 
-    for k in range(4):
-        for half in range(2):
-            mixed = sum(
-                (STAGE_WEIGHT[k] * mixes[k][t]) * rate[t][half]
-                for t in range(3)
-                if mixes[k][t] != 0.0
-            )
-            for spin in range(2):
-                par[4 * k + 2 * half + spin] = column(mixed[spin : spin + 1, :])
     par[16] = column(wt[...])
     par[17] = column(lead[...].astype(jnp.float32))
 
@@ -505,6 +472,39 @@
 
         lax.fori_loop(0, chunks // unroll, body, 0)
 
+    group = grp[...]
+    energy_row = en[...]
+    energy = jnp.zeros(group.shape, jnp.float32)
+    for g in range(energy_row.shape[1]):
+        energy = energy + jnp.where(group == g, energy_row[:, g : g + 1], 0.0)
+    amp_re = amp[0:2, :]
+    amp_im = amp[2:4, :]
+    rate = []
+    for offset in (0.0, 0.5 * time_step, time_step):
+        phase = energy * (start_time + offset)
+        cosine = jnp.cos(phase)
+        sine = jnp.sin(phase)
+        rate.append(
+            (
+                amp_im * cosine - amp_re * sine,
+                -(amp_re * cosine + amp_im * sine),
+            )
+        )
+    mixes = [
+        [time_step / 6.0, 4.0 * time_step / 6.0, time_step / 6.0],
+        [time_step / 6.0, 2.0 * time_step / 6.0, 0.0],
+        [time_step / 6.0, time_step / 6.0, 0.0],
+        [time_step / 4.0, 0.0, 0.0],
+    ]
+    for k in range(4):
+        for half in range(2):
+            mixed = sum(
+                (STAGE_WEIGHT[k] * mixes[k][t]) * rate[t][half]
+                for t in range(3)
+                if mixes[k][t] != 0.0
+            )
+            for spin in range(2):
+                par[4 * k + 2 * half + spin] = column(mixed[spin : spin + 1, :])
     def terms(block, carry):
         for u in range(unroll):
             site_terms(block * unroll + u)

time: 17.1 us -> 17.1 us (level)
  no operation moved by 1% of the time
where the time goes in v6:
time: 17.1 us; the launch traced here: 16.9 us
  Pallas kernels  16.3 us (95%)
  between operations  0.64 us (4%)
    pallas_call x1, Pallas kernels, local(): pl.pallas_call(functools.partial(kernel, nm, ns, sites), out_shape=(jax.S...  15.4 us
    pallas_call x1, Pallas kernels, local(): pl.pallas_call(hand_out, out_shape=tuple((jax.ShapeDtypeStruct(x.shape, f...  0.87 us

profile of v6, /device:TPU:1, one launch (start us, length us, event | category | flops | bytes accessed | tf_op | source)
XLA Modules:
  0.0 16.9 jit_solution(1543102182259378995)
XLA Ops:
  0.6 15.4 %shard_map.121 = (f32[4,8,4096]{2,1,0:T(8,128)S(1)}, f32[5,4096]{1,0:T(8,128)S(1)}, f32[3,4096]{1,0:T(4,128)S(1)}) custom-call(f32[4,8,4096]{2,1,0:T(8,128)} %wave_hbm.1, f32[32,128]{1,0:T(8,128)} %bitcast.7, f32[32,128]{1,0:T(8,128)} %bitcast.8, f32[3,4096]{1,0:T(4,128)} %mag_hbm.1, s32[32,128]{1,0:T(8,128)} %bitcast.9, f32[1,8]{1,0:T(1,128)} %bitcast.10, ...), custom_call_target="tpu_custom_call" | custom-call | tf_op jit(solution)/shard_map/pallas_call | solution.py:750
  16.0 0.9 %shard_map.122 = (f32[4,8,4096]{2,1,0:T(8,128)}, f32[5,4096]{1,0:T(8,128)}, f32[3,4096]{1,0:T(4,128)}) custom-call(f32[4,8,4096]{2,1,0:T(8,128)S(1)} %get-tuple-element.6.next_v, f32[5,4096]{1,0:T(8,128)S(1)} %get-tuple-element.7.dens_v, f32[3,4096]{1,0:T(4,128)S(1)} %get-tuple-element.8.magn_v), custom_call_target="tpu_custom_call" | custom-call | tf_op jit(solution)/shard_map/pallas_call | solution.py:830
